TPU v7x, 32 devices: a whole 2x2x4 slice. The times are simulated.
32 devices in a mesh: grp: 4 (over z), dev: 8 (over y, x, core).
Axes of the slice: x: 2, y: 2, z: 4, core: 2. Of those that a mesh axis runs over, the one named last changes fastest.
Arguments:
- velocity_old: float32 [128, 3, 32, 1024], P(('grp', 'dev')), may hold values from -6 to 6
- viscosity_old: float32 [128, 32, 1024], P(('grp', 'dev')), may hold values from 0.25 to 4
- source: int32 [128], replicated, may hold values from 0 to 127, as said below
Outputs:
- velocity_new: float32 [128, 3, 32, 1024], P(('grp', 'dev'))
Inputs may be any that keep to these rules, and one draw needn't show every extreme that they name: `source`: A permutation; the old block of new block b lies in the same agglomeration group and has the same place among its device's 4 blocks; the 4 blocks of a new device come from 4 different old devices of its group, and each old device sends 1 block to each of 4 different new devices.
All inputs are finite; a program needn't handle non-finite values.
Results may differ from a plain program's by a relative error of at most 0.0001.
Values sent between devices are 32-bit elements; how exact they have to be, the bound alone decides.
No kernel may reach another device: no remote copies, remote signals or barrier semaphores. Data moves between devices by JAX's collectives and lax.ppermute only.
A program may use at most 256 MiB of HBM per device.

v0:
```python
import math

import jax
import jax.numpy as jnp
from jax import lax
from jax.sharding import PartitionSpec as P

SWEEPS = 2
BOTTOM = 8


RELAX_WEIGHT = 0.8
DIFFUSION_NUMBER = 1000.0


def padded_2(cells, sides, width):
    for axis, dim in sides:
        count = lax.axis_size(axis)
        ends = count - 1
        head = lax.slice_in_dim(cells, 0, width, axis=dim)
        tail = lax.slice_in_dim(cells, cells.shape[dim] - width, cells.shape[dim], axis=dim)
        cells = jnp.concatenate(
            [
                lax.ppermute(tail, axis, [(i, (i + 1) % count) for i in range(ends)]),
                cells,
                lax.ppermute(head, axis, [((i + 1) % count, i) for i in range(ends)]),
            ],
            axis=dim,
        )
    return cells


def blocks_to_grid(blocks):
    num_blocks, channels, edge_len = (blocks.shape[0], blocks.shape[1], blocks.shape[2])
    columns = num_blocks // 4
    parted = blocks.reshape(columns, 2, 2, channels, edge_len, edge_len, edge_len)
    parted = parted.transpose(3, 0, 6, 1, 4, 2, 5)
    return parted.reshape(channels, columns * edge_len, 4 * edge_len * edge_len)


def grid_to_blocks(grid):
    channels, length, plane = grid.shape
    edge_len = math.isqrt(plane) // 2
    columns = length // edge_len
    parted = grid.reshape(channels, columns, edge_len, 2, edge_len, 2, edge_len)
    parted = parted.transpose(1, 3, 5, 0, 4, 6, 2)
    return parted.reshape(columns * 4, channels, edge_len, edge_len * edge_len)


def flat_neighbors(array):
    plane = array.shape[2]
    width_y = math.isqrt(plane)
    middle = array[:, 1:-1]
    padded = jnp.pad(middle, ((0, 0), (0, 0), (width_y, width_y)))
    column = jnp.arange(plane) % width_y
    lower_y = jnp.where(column == 0, 0.0, padded[:, :, width_y - 1 : width_y - 1 + plane])
    upper_y = jnp.where(column == width_y - 1, 0.0, padded[:, :, width_y + 1 : width_y + 1 + plane])
    return (
        middle,
        (
            array[:, :-2],
            array[:, 2:],
            padded[:, :, 0:plane],
            padded[:, :, 2 * width_y : 2 * width_y + plane],
            lower_y,
            upper_y,
        ),
    )


def coefficients(viscous, level_coef, pad_along):
    middle, beside_all = flat_neighbors(pad_along(viscous))
    face_coef = tuple((0.5 * (middle + neighbor) for neighbor in beside_all))
    summed = face_coef[0] + face_coef[1] + face_coef[2] + face_coef[3] + face_coef[4] + face_coef[5]
    diagonal = 1.0 + level_coef * summed
    return (face_coef, diagonal)


def operate(solution, face_coef, diagonal, level_coef, pad_along):
    middle, beside_all = flat_neighbors(pad_along(solution))
    summed = face_coef[0] * beside_all[0]
    for index_no in range(1, 6):
        summed = summed + face_coef[index_no] * beside_all[index_no]
    return diagonal * solution - level_coef * summed


def smooth(solution, right_side, face_coef, diagonal, level_coef, pad_along, repeats):
    for sweep_no in range(repeats):
        solution = (
            solution
            + RELAX_WEIGHT
            * (right_side - operate(solution, face_coef, diagonal, level_coef, pad_along))
            / diagonal
        )
    return solution


def coarsen(grid):
    channels, length, plane = grid.shape
    width_y = math.isqrt(plane)
    shaped = grid.reshape(channels, length // 2, 2, width_y // 2, 2, width_y // 2, 2)
    return shaped.mean(axis=(2, 4, 6)).reshape(channels, length // 2, plane // 4)


def refine(grid):
    channels, length, plane = grid.shape
    width_y = math.isqrt(plane)
    shaped = grid.reshape(channels, length, 1, width_y, 1, width_y, 1)
    shaped = jnp.broadcast_to(shaped, (channels, length, 2, width_y, 2, width_y, 2))
    return shaped.reshape(channels, 2 * length, 4 * plane)


def cell_pad(array):
    return padded_2(array, ((("grp", "dev"), 1),), 1)


def group_pad(array):
    return padded_2(array, (("grp", 1),), 1)


def group_bottom(level_rhs, viscous):
    stacked = jnp.concatenate([level_rhs, viscous], axis=0)
    gathered = lax.all_gather(stacked, "dev", axis=1, tiled=True)
    group_rhs = gathered[:3]
    group_visc = gathered[3:]
    level_coef = DIFFUSION_NUMBER / 64.0
    face_coef, diagonal = coefficients(group_visc, level_coef, group_pad)
    solved = smooth(
        jnp.zeros_like(group_rhs), group_rhs, face_coef, diagonal, level_coef, group_pad, BOTTOM
    )
    own_width = level_rhs.shape[1]
    return lax.dynamic_slice_in_dim(solved, lax.axis_index("dev") * own_width, own_width, 1)


def vcycle_solve(right_side, viscous):
    stored = []
    solution = right_side
    level_rhs = right_side
    for level_no in range(3):
        level_coef = DIFFUSION_NUMBER / 4.0**level_no
        face_coef, diagonal = coefficients(viscous, level_coef, cell_pad)
        solution = smooth(solution, level_rhs, face_coef, diagonal, level_coef, cell_pad, SWEEPS)
        residue = level_rhs - operate(solution, face_coef, diagonal, level_coef, cell_pad)
        stored.append((solution, level_rhs, face_coef, diagonal, level_coef))
        level_rhs = coarsen(residue)
        viscous = coarsen(viscous)
        solution = jnp.zeros_like(level_rhs)
    solution = group_bottom(level_rhs, viscous)
    for level_no in (2, 1, 0):
        before, level_rhs, face_coef, diagonal, level_coef = stored[level_no]
        solution = smooth(
            before + refine(solution), level_rhs, face_coef, diagonal, level_coef, cell_pad, SWEEPS
        )
    return solution


def local(velocity_old, viscosity_old, source):
    group_index = lax.axis_index("grp")
    member_index = lax.axis_index("dev")
    member_count = lax.axis_size("dev")
    blk_per = velocity_old.shape[0]
    group_base = group_index * member_count * blk_per
    src_table = (
        lax.dynamic_slice_in_dim(source, group_base, member_count * blk_per).reshape(
            member_count, blk_per
        )
        - group_base
    )
    from_dev = src_table // blk_per
    from_slot = src_table % blk_per
    mine_dev = lax.dynamic_index_in_dim(from_dev, member_index, 0, keepdims=False)
    mine_slot = lax.dynamic_index_in_dim(from_slot, member_index, 0, keepdims=False)
    wanted = mine_dev * blk_per + mine_slot
    pieces = (
        lax.all_gather(velocity_old, "dev", axis=0, tiled=True),
        lax.all_gather(viscosity_old, "dev", axis=0, tiled=True),
    )
    piece_rows = pieces[0].shape[0]
    inside = (wanted >= 0) & (wanted < piece_rows)
    clipped = jnp.clip(wanted, 0, piece_rows - 1)
    new_vel = jnp.where(
        inside[:, None, None, None],
        jnp.take(pieces[0], clipped, axis=0),
        jnp.zeros_like(velocity_old),
    )
    new_visc = jnp.where(
        inside[:, None, None], jnp.take(pieces[1], clipped, axis=0), jnp.zeros_like(viscosity_old)
    )
    right_side = blocks_to_grid(new_vel)
    viscous = blocks_to_grid(new_visc[:, None])
    solution = vcycle_solve(right_side, viscous)
    return grid_to_blocks(solution)


def solution(mesh):
    return jax.shard_map(
        local,
        mesh=mesh,
        in_specs=(P(("grp", "dev"), None, None, None), P(("grp", "dev"), None, None), P()),
        out_specs=P(("grp", "dev"), None, None, None),
        check_vma=False,
    )
```

profile of v0, /device:TPU:7, one launch (start us, length us, event | category | flops | bytes accessed | tf_op | source)
XLA Modules:
  0.0 862.6 jit_solution(11526730936189897904)
XLA Ops:
  11.2 4.8 collective-permute-start.18
  19.5 27.3 %all-gather.5.cloned.1.call-done = f32[32,32,1024]{2,1,0:T(8,128)} async-done(((f32[4,32,1024]{2,1,0:T(8,128)}), f32[32,32,1024]{2,1,0:T(8,128)}) %all-gather.5.cloned.1.call-update) | async-done | bytes 4194320 | tf_op jit(solution)/shard_map/all_gather | solution.py:176
  54.9 21.9 %reshape_reshape.2 = f32[16,2,32,2,32,2]{1,0,5,4,3,2:T(8,128)} reshape(f32[1,1,32,2,32,2,32]{2,6,5,4,3,1,0:T(8,128)} %fusion.454) | data formatting | bytes 1048576 | tf_op jit(solution)/shard_map/reshape;reshape | solution.py:101
  76.9 13.8 %reduce_sum.55 = f32[16,32,32]{0,2,1:T(8,128)S(1)} reduce(f32[16,2,32,2,32,2]{1,0,5,4,3,2:T(8,128)} %reshape_reshape.2, f32[]{:T(128)} %constant.249.clone.1), dimensions={1,3,5}, to_apply=%region_1.2 | reduce | flops 114688 | bytes 589828 | tf_op jit(solution)/shard_map/reduce_sum | solution.py:102
  110.5 10.6 %all-gather.3.cloned.1.call-done = f32[32,3,32,1024]{3,2,1,0:T(8,128)} async-done(((f32[4,3,32,1024]{3,2,1,0:T(8,128)}), f32[32,3,32,1024]{3,2,1,0:T(8,128)}) %all-gather.3.cloned.1.call-update) | async-done | bytes 12582928 | tf_op jit(solution)/shard_map/all_gather | solution.py:175
  121.0 5.2 gather_fusion
  130.3 10.0 %copy.71 = f32[1,2,2,3,32,32,32]{5,2,4,1,6,3,0:T(2,128)} copy(f32[1,2,2,3,32,32,32]{6,5,4,3,2,1,0:T(8,128)} %gather.13) | data formatting | bytes 3145728 | tf_op jit(solution)/shard_map/jit(_take)/gather | solution.py:183
  140.3 11.8 %select_bitcast_fusion = f32[3,1,32,2,32,2,32]{6,5,4,3,2,0,1:T(2,128)} fusion(f32[1,2,2,3,32,32,32]{5,2,4,1,6,3,0:T(2,128)} %copy.71, pred[2,2]{1,0:T(4,128)(4,1)S(1)} %compare_and_fusion, pred[2,2]{1,0:T(4,128)(4,1)S(1)} %and.182), kind=kLoop, calls=%fused_computation.2 | loop fusion | flops 786432 | bytes 3145736 | tf_op jit(solution)/shard_map/transpose | solution.py:37
  152.1 9.5 %reshape.248 = f32[3,32,4096]{2,1,0:T(8,128)S(1)} reshape(f32[3,1,32,2,32,2,32]{6,5,4,3,2,0,1:T(2,128)} %select_bitcast_fusion) | data formatting | bytes 3145728 | tf_op jit(solution)/shard_map/reshape | solution.py:38
  167.8 5.2 add_bitcast_fusion
  173.1 5.4 collective-permute-start.8
  182.5 5.4 collective-permute-start.4
  190.7 4.5 collective-permute-done.5
  202.5 4.9 collective-permute-start.10
  212.6 153.9 %reshape.250 = f32[3,16,2,32,2,32,2]{6,5,4,3,2,1,0:T(8,128)} reshape(f32[3,32,4096]{2,1,0:T(8,128)} %fusion.35) | data formatting | bytes 3145728 | tf_op jit(solution)/shard_map/reshape | solution.py:101
  366.5 31.6 %reduce_sum.54 = f32[3,16,32,32]{3,2,1,0:T(8,128)} reduce(f32[3,16,2,32,2,32,2]{6,5,4,3,2,1,0:T(8,128)} %reshape.250, f32[]{:T(128)} %constant.249.clone.1), dimensions={2,4,6}, to_apply=%region_0.1 | reduce | flops 344064 | bytes 1769476 | tf_op jit(solution)/shard_map/reduce_sum | solution.py:102
  405.7 5.0 collective-permute-start.12
  429.3 14.7 %reshape.251 = f32[3,8,2,16,2,16,2]{6,5,4,3,2,1,0:T(8,128)} reshape(f32[3,16,1024]{2,1,0:T(8,128)} %fusion.106) | data formatting | bytes 393216 | tf_op jit(solution)/shard_map/reshape | solution.py:101
  443.9 6.3 reduce_sum.56
  461.2 4.6 collective-permute-start.26
  471.6 5.3 collective-permute-start.22
  492.2 8.0 all_gather.11
  564.6 12.4 %collective-permute-start.42 = (f32[3,1,256]{2,1,0:T(1,128)S(1)}, f32[3,1,256]{2,1,0:T(1,128)S(1)}, u32[]{:S(2)}, u32[]{:S(2)}) collective-permute-start(f32[3,1,256]{2,1,0:T(1,128)S(1)} %get-tuple-element.73), channel_id=1, source_target_pairs={{0,1},{1,2},{2,3},{3,4},{4,5},{5,6},{6,7},{7,8},{8,9},{9,10},{10,1... | collective-permute-start | bytes 9224 | tf_op jit(solution)/shard_map/ppermute | solution.py:24
  578.9 4.8 collective-permute-done.43
  596.0 5.7 broadcast_in_dim.360
  601.7 10.4 %reshape.254 = f32[3,16,1024]{2,1,0:T(8,128)} reshape(f32[3,8,2,16,2,16,2]{6,5,4,3,2,1,0:T(8,128)} %broadcast_in_dim.360) | data formatting | bytes 393216 | tf_op jit(solution)/shard_map/reshape | solution.py:110
  635.1 32.2 %broadcast_in_dim.362 = f32[3,16,2,32,2,32,2]{6,5,4,3,2,1,0:T(8,128)} broadcast(f32[3,16,32,32]{3,2,1,0:T(8,128)} %broadcast_in_dim.361), dimensions={0,1,3,5} | broadcast | bytes 1769472 | tf_op jit(solution)/shard_map/broadcast_in_dim | solution.py:109
  667.3 138.6 %reshape.255 = f32[3,32,4096]{2,1,0:T(8,128)} reshape(f32[3,16,2,32,2,32,2]{6,5,4,3,2,1,0:T(8,128)} %broadcast_in_dim.362) | data formatting | bytes 3145728 | tf_op jit(solution)/shard_map/reshape | solution.py:110
  812.6 4.8 collective-permute-done.51
  831.6 7.7 reshape.256
  839.4 10.0 %copy.78 = f32[1,2,2,3,32,32,32]{6,5,4,3,2,1,0:T(8,128)} copy(f32[1,2,2,3,32,32,32]{5,2,4,1,6,3,0:T(2,128)} %bitcast.84) | data formatting | bytes 3145728 | tf_op jit(solution)/shard_map/transpose | solution.py:46
  849.4 5.9 reshape.257
  (337 shorter events, 244.8 us)
Async XLA Ops:
  6.5 40.3 %all-gather.5.cloned.1.call-start = ((), (), s32[]{:S(2)}) async-start(), calls=%async_computation.1 | async-start | bytes 4718592 | tf_op jit(solution)/shard_map/all_gather | solution.py:176
  7.3 113.8 %all-gather.3.cloned.1.call-start = ((), (), s32[]{:S(2)}) async-start(), calls=%async_computation | async-start | bytes 14155776 | tf_op jit(solution)/shard_map/all_gather | solution.py:175
  8.6 444.3 %collective-permute-start.19 = (f32[3,1,256]{2,1,0:T(1,128)}, f32[3,1,256]{2,1,0:T(1,128)}, u32[]{:S(2)}, u32[]{:S(2)}) collective-permute-start(f32[3,1,256]{2,1,0:T(1,128)} %broadcast.449), channel_id=1, source_target_pairs={{1,0},{2,1},{3,2},{4,3},{5,4},{6,5},{7,6},{8,7},{9,8},{10,9},{11,1... | collective-permute-start | bytes 9224 | tf_op jit(solution)/shard_map/ppermute | solution.py:26
  11.2 441.7 %collective-permute-start.18 = (f32[3,1,256]{2,1,0:T(1,128)}, f32[3,1,256]{2,1,0:T(1,128)}, u32[]{:S(2)}, u32[]{:S(2)}) collective-permute-start(f32[3,1,256]{2,1,0:T(1,128)} %broadcast.449), channel_id=1, source_target_pairs={{0,1},{1,2},{2,3},{3,4},{4,5},{5,6},{6,7},{7,8},{8,9},{9,10},{10,1... | collective-permute-start | bytes 9224 | tf_op jit(solution)/shard_map/ppermute | solution.py:24
  16.6 385.2 %collective-permute-start.11 = (f32[3,1,1024]{2,1,0:T(1,128)}, f32[3,1,1024]{2,1,0:T(1,128)}, u32[]{:S(2)}, u32[]{:S(2)}) collective-permute-start(f32[3,1,1024]{2,1,0:T(1,128)} %broadcast.445), channel_id=1, source_target_pairs={{1,0},{2,1},{3,2},{4,3},{5,4},{6,5},{7,6},{8,7},{9,8},{10,9},{11,1... | collective-permute-start | bytes 36872 | tf_op jit(solution)/shard_map/ppermute | solution.py:26
  100.4 61.4 %collective-permute-start = (f32[1,1,4096]{2,1,0:T(1,128)S(1)}, f32[1,1,4096]{2,1,0:T(1,128)S(1)}, u32[]{:S(2)}, u32[]{:S(2)}) collective-permute-start(f32[1,1,4096]{2,1,0:T(1,128)S(1)} %get-tuple-element.35), channel_id=1, source_target_pairs={{0,1},{1,2},{2,3},{3,4},{4,5},{5,6},{6,7},{7,8},{8,9},{9,10},{10,1... | collective-permute-start | bytes 49160 | tf_op jit(solution)/shard_map/ppermute | solution.py:24
  104.7 61.2 %collective-permute-start.1 = (f32[1,1,4096]{2,1,0:T(1,128)S(1)}, f32[1,1,4096]{2,1,0:T(1,128)S(1)}, u32[]{:S(2)}, u32[]{:S(2)}) collective-permute-start(f32[1,1,4096]{2,1,0:T(1,128)S(1)} %get-tuple-element.36), channel_id=1, source_target_pairs={{1,0},{2,1},{3,2},{4,3},{5,4},{6,5},{7,6},{8,7},{9,8},{10,9},{11,1... | collective-permute-start | bytes 49160 | tf_op jit(solution)/shard_map/ppermute | solution.py:26
  161.7 11.3 %collective-permute-start.2 = (f32[3,1,4096]{2,1,0:T(1,128)S(1)}, f32[3,1,4096]{2,1,0:T(1,128)S(1)}, u32[]{:S(2)}, u32[]{:S(2)}) collective-permute-start(f32[3,1,4096]{2,1,0:T(1,128)S(1)} %get-tuple-element.26), channel_id=1, source_target_pairs={{0,1},{1,2},{2,3},{3,4},{4,5},{5,6},{6,7},{7,8},{8,9},{9,10},{10,1... | collective-permute-start | bytes 147464 | tf_op jit(solution)/shard_map/ppermute | solution.py:24
  165.9 12.6 %collective-permute-start.3 = (f32[3,1,4096]{2,1,0:T(1,128)S(1)}, f32[3,1,4096]{2,1,0:T(1,128)S(1)}, u32[]{:S(2)}, u32[]{:S(2)}) collective-permute-start(f32[3,1,4096]{2,1,0:T(1,128)S(1)} %get-tuple-element.27), channel_id=1, source_target_pairs={{1,0},{2,1},{3,2},{4,3},{5,4},{6,5},{7,6},{8,7},{9,8},{10,9},{11,1... | collective-permute-start | bytes 147464 | tf_op jit(solution)/shard_map/ppermute | solution.py:26
  173.1 9.4 %collective-permute-start.8 = (f32[1,1,1024]{2,1,0:T(1,128)S(1)}, f32[1,1,1024]{2,1,0:T(1,128)S(1)}, u32[]{:S(2)}, u32[]{:S(2)}) collective-permute-start(f32[1,1,1024]{2,1,0:T(1,128)S(1)} %get-tuple-element.69), channel_id=1, source_target_pairs={{0,1},{1,2},{2,3},{3,4},{4,5},{5,6},{6,7},{7,8},{8,9},{9,10},{10,1... | collective-permute-start | bytes 12296 | tf_op jit(solution)/shard_map/ppermute | solution.py:24
  178.5 9.4 %collective-permute-start.9 = (f32[1,1,1024]{2,1,0:T(1,128)S(1)}, f32[1,1,1024]{2,1,0:T(1,128)S(1)}, u32[]{:S(2)}, u32[]{:S(2)}) collective-permute-start(f32[1,1,1024]{2,1,0:T(1,128)S(1)} %get-tuple-element.70), channel_id=1, source_target_pairs={{1,0},{2,1},{3,2},{4,3},{5,4},{6,5},{7,6},{8,7},{9,8},{10,9},{11,1... | collective-permute-start | bytes 12296 | tf_op jit(solution)/shard_map/ppermute | solution.py:26
  182.5 8.2 collective-permute-start.4
  188.0 7.2 collective-permute-start.5
  199.3 8.2 collective-permute-start.7
  202.5 201.9 %collective-permute-start.10 = (f32[3,1,1024]{2,1,0:T(1,128)}, f32[3,1,1024]{2,1,0:T(1,128)}, u32[]{:S(2)}, u32[]{:S(2)}) collective-permute-start(f32[3,1,1024]{2,1,0:T(1,128)} %broadcast.445), channel_id=1, source_target_pairs={{0,1},{1,2},{2,3},{3,4},{4,5},{5,6},{6,7},{7,8},{8,9},{9,10},{10,1... | collective-permute-start | bytes 36872 | tf_op jit(solution)/shard_map/ppermute | solution.py:24
  207.4 203.2 %collective-permute-start.16 = (f32[1,1,256]{2,1,0:T(1,128)}, f32[1,1,256]{2,1,0:T(1,128)}, u32[]{:S(2)}, u32[]{:S(2)}) collective-permute-start(f32[1,1,256]{2,1,0:T(1,128)} %get-tuple-element.85), channel_id=1, source_target_pairs={{0,1},{1,2},{2,3},{3,4},{4,5},{5,6},{6,7},{7,8},{8,9},{9,10},{10,1... | collective-permute-start | bytes 3080 | tf_op jit(solution)/shard_map/ppermute | solution.py:24
  401.8 10.8 %collective-permute-start.17 = (f32[1,1,256]{2,1,0:T(1,128)}, f32[1,1,256]{2,1,0:T(1,128)S(1)}, u32[]{:S(2)}, u32[]{:S(2)}) collective-permute-start(f32[1,1,256]{2,1,0:T(1,128)} %get-tuple-element.86), channel_id=1, source_target_pairs={{1,0},{2,1},{3,2},{4,3},{5,4},{6,5},{7,6},{8,7},{9,8},{10,9},{11,1... | collective-permute-start | bytes 3080 | tf_op jit(solution)/shard_map/ppermute | solution.py:26
  405.7 8.3 collective-permute-start.12
  410.7 6.8 collective-permute-start.13
  420.7 6.8 collective-permute-start.15
  455.0 14.3 %collective-permute-start.20 = (f32[3,1,256]{2,1,0:T(1,128)}, f32[3,1,256]{2,1,0:T(1,128)}, u32[]{:S(2)}, u32[]{:S(2)}) collective-permute-start(f32[3,1,256]{2,1,0:T(1,128)} %get-tuple-element.77), channel_id=1, source_target_pairs={{0,1},{1,2},{2,3},{3,4},{4,5},{5,6},{6,7},{7,8},{8,9},{9,10},{10,1... | collective-permute-start | bytes 9224 | tf_op jit(solution)/shard_map/ppermute | solution.py:24
  457.2 12.1 %collective-permute-start.21 = (f32[3,1,256]{2,1,0:T(1,128)}, f32[3,1,256]{2,1,0:T(1,128)}, u32[]{:S(2)}, u32[]{:S(2)}) collective-permute-start(f32[3,1,256]{2,1,0:T(1,128)} %get-tuple-element.78), channel_id=1, source_target_pairs={{1,0},{2,1},{3,2},{4,3},{5,4},{6,5},{7,6},{8,7},{9,8},{10,9},{11,1... | collective-permute-start | bytes 9224 | tf_op jit(solution)/shard_map/ppermute | solution.py:26
  459.9 48.6 %collective-permute-start.27 = (f32[3,1,64]{2,0,1:T(4,128)}, f32[3,1,64]{2,0,1:T(4,128)}, u32[]{:S(2)}, u32[]{:S(2)}) collective-permute-start(f32[3,1,64]{2,0,1:T(4,128)} %broadcast.453), channel_id=1, source_target_pairs={{8,0},{16,8},{24,16},{9,1},{17,9},{25,17},{10,2},{18,10},{26,18},{... | collective-permute-start | bytes 2312 | tf_op jit(solution)/shard_map/ppermute | solution.py:26
  461.2 47.3 %collective-permute-start.26 = (f32[3,1,64]{2,0,1:T(4,128)}, f32[3,1,64]{2,0,1:T(4,128)}, u32[]{:S(2)}, u32[]{:S(2)}) collective-permute-start(f32[3,1,64]{2,0,1:T(4,128)} %broadcast.453), channel_id=1, source_target_pairs={{0,8},{8,16},{16,24},{1,9},{9,17},{17,25},{2,10},{10,18},{18,26},{... | collective-permute-start | bytes 2312 | tf_op jit(solution)/shard_map/ppermute | solution.py:24
  471.6 10.1 %collective-permute-start.22 = (f32[3,1,256]{2,1,0:T(1,128)}, f32[3,1,256]{2,1,0:T(1,128)}, u32[]{:S(2)}, u32[]{:S(2)}) collective-permute-start(f32[3,1,256]{2,1,0:T(1,128)} %get-tuple-element.75), channel_id=1, source_target_pairs={{0,1},{1,2},{2,3},{3,4},{4,5},{5,6},{6,7},{7,8},{8,9},{9,10},{10,1... | collective-permute-start | bytes 9224 | tf_op jit(solution)/shard_map/ppermute | solution.py:24
  476.9 7.0 collective-permute-start.23
  564.6 14.3 %collective-permute-start.42 = (f32[3,1,256]{2,1,0:T(1,128)S(1)}, f32[3,1,256]{2,1,0:T(1,128)S(1)}, u32[]{:S(2)}, u32[]{:S(2)}) collective-permute-start(f32[3,1,256]{2,1,0:T(1,128)S(1)} %get-tuple-element.73), channel_id=1, source_target_pairs={{0,1},{1,2},{2,3},{3,4},{4,5},{5,6},{6,7},{7,8},{8,9},{9,10},{10,1... | collective-permute-start | bytes 9224 | tf_op jit(solution)/shard_map/ppermute | solution.py:24
  576.9 6.7 collective-permute-start.43
  615.2 6.8 collective-permute-start.47
  625.2 6.8 collective-permute-start.49
  810.2 7.2 collective-permute-start.51
  821.5 7.2 collective-permute-start.53
  (86 other events, 3046.9 us)
Sparse Core Ops, SparseCore 0:
  9.2 37.5 all-gather.4
  48.7 72.2 all-gather.2
where the time goes:
time: 871 us; the launch traced here: 863 us
  local copies, waits for them, and re-layouts  466 us (54%)
  starting transfers between devices  144 us (17%)
  other arithmetic  126 us (14%)
  waiting for transfers between devices  103 us (12%)
  between operations  15.6 us (2%)
    reshape x3, local copies, waits for them, and re-layouts, coarsen(): grid.reshape(channels, length // 2, 2, width_y // 2, 2, width_y // 2, 2)  172 us
    reshape x3, local copies, waits for them, and re-layouts, refine(): return shaped.reshape(channels, 2 * length, 4 * plane)  152 us
    ppermute x27, starting transfers between devices, padded_2(): lax.ppermute(tail, axis, [(i, (i + 1) % count) for i in range(ends)])  91.7 us
    ppermute x27, waiting for transfers between devices, padded_2(): lax.ppermute(head, axis, [((i + 1) % count, i) for i in range(ends)])  64.2 us
    reduce_sum x6, other arithmetic, coarsen(): shaped.mean(axis=(2, 4, 6)).reshape(channels, length // 2, plane // 4)  58.2 us
    ppermute x27, starting transfers between devices, padded_2(): lax.ppermute(head, axis, [((i + 1) % count, i) for i in range(ends)])  52.2 us
    broadcast_in_dim x6, local copies, waits for them, and re-layouts, refine(): jnp.broadcast_to(shaped, (channels, length, 2, width_y, 2, width_y, 2))  44.5 us
    all_gather x1, waiting for transfers between devices, local(): lax.all_gather(viscosity_old, 'dev', axis=0, tiled=True)  27.3 us
  transfers between devices with their start and end apart: 56, of which 20 were waited for; matrix products, arithmetic and copies ran while one was open for 41% of the time, Pallas kernels for 0%

commit v1 on v0

v1 whole, which is shorter than its diff:
```python
import functools

import jax
import jax.numpy as jnp
from jax import lax
from jax.experimental import pallas as pl
from jax.experimental.pallas import tpu as pltpu
from jax.sharding import PartitionSpec as P


BOTTOM = 8
DIFFUSION_NUMBER = 1000.0
WEIGHT = 0.8
LANES = 128
MID = 8
F32 = jnp.float32
ANY = pl.BlockSpec(memory_space=pl.ANY)
WHOLE = pl.BlockSpec(memory_space=pltpu.VMEM)
SCALARS = pl.BlockSpec(memory_space=pltpu.SMEM)

HALO = 7
BASE0 = 8
BASE1 = 4
SIDE0 = 2
SIDE1 = 3
FETCHED = SIDE1 - 1
EDGES = 3 * FETCHED
REACH = 3
MEGA = 1024 * 1024


def iota(shape, axis):
    return lax.broadcasted_iota(jnp.int32, shape, axis)


def spin(value, shift, axis):
    size = value.shape[axis]
    return pltpu.roll(value, shift % size, axis)


def beside0(v):
    row = iota((MID, LANES), 0)
    low = spin(v[3 * MID :], 1, 0)
    low = jnp.where(row == 0, spin(low, 64, 1), low)
    high = spin(v[:MID], -1, 0)
    high = jnp.where(row == MID - 1, spin(high, 64, 1), high)
    return (
        jnp.concatenate([low, v[: 3 * MID]], axis=0),
        jnp.concatenate([v[MID:], high], axis=0),
        spin(v, 1, 1),
        spin(v, -1, 1),
    )


def beside1(v):
    row, lane = iota(v.shape, 0), iota(v.shape, 1)
    other = spin(v, 64, 1)
    down, up = spin(other, 1, 0), spin(other, -1, 0)
    down = jnp.where(row == 0, spin(down, 32, 1), down)
    up = jnp.where(row == MID - 1, spin(up, -32, 1), up)
    return (jnp.where(lane < 64, down, other), jnp.where(lane < 64, other, up), spin(v, 1, 1), spin(v, -1, 1))


def beside_packed(v, width):
    row = iota(v.shape, 0)
    down, up = spin(v, width, 0), spin(v, -width, 0)
    down = jnp.where(row < width, spin(down, 16, 1), down)
    up = jnp.where(row >= MID - width, spin(up, -16, 1), up)
    return (down, up, spin(v, width, 1), spin(v, -width, 1))


def beside2(v):
    return beside_packed(v, 1)


def beside3(v):
    return beside_packed(v, 2)


def outside(level):
    shape = (4 * MID if level == 0 else MID, LANES)
    row, lane = iota(shape, 0), iota(shape, 1)
    if level == 0:
        z = lane & 63
        return (row == 0) & (lane < 64), (row == 4 * MID - 1) & (lane >= 64), z == 0, z == 63
    if level == 1:
        z = lane & 31
        return (row == 0) & (lane < 32), (row == MID - 1) & (lane >= 96), z == 0, z == 31
    width = level - 1
    z, side = lane & 15, lane & 31
    return (row < width) & (side < 16), (row >= MID - width) & (side >= 16), z < width, z >= 16 - width


def over_layers(low, high, step, work):
    turns = (high - low) // step

    def body(t, _):
        for d in range(step):
            work(low + t * step + d)
        return 0

    if turns == 1:
        body(0, 0)
    else:
        lax.fori_loop(0, turns, body, 0)
    for i in range(low + turns * step, high):
        work(i)


def make_weights(level, beside, nu, coef, scale, back, low, high, first_x, total_x, step=2):
    level_coef = DIFFUSION_NUMBER / 4.0**level

    def work(i):
        mid = nu[i]
        out = outside(level)
        others = [nu[i - 1], nu[i + 1]] + [jnp.where(far, 0.0, v) for far, v in zip(out, beside(mid))]
        faces = [0.5 * (mid + other) for other in others]
        diag = 1.0 + level_coef * (faces[0] + faces[1] + faces[2] + faces[3] + faces[4] + faces[5])
        x = first_x + i
        weight = jnp.where((x >= 0) & (x < total_x), WEIGHT, 0.0)
        own = weight / diag
        scale[i] = own
        if back is not None:
            back[i] = diag * (1.0 / WEIGHT)
        own = own * level_coef
        for at, face in enumerate(faces):
            value = own * face
            coef[at, i] = value if at < 2 else jnp.where(out[at - 2], 0.0, value)

    over_layers(low, high, step, work)


def gathered_sum(beside, src, c, i, coef_i):
    mid = src[c, i]
    y_low, y_high, z_low, z_high = beside(mid)
    total = coef_i[0] * src[c, i - 1] + coef_i[1] * src[c, i + 1]
    total = total + (coef_i[2] * y_low + coef_i[3] * y_high)
    total = total + (coef_i[4] * z_low + coef_i[5] * z_high)
    return mid, total


def sweep(beside, src, dst, coef, right, comps, low, high, step=2, scale=None):
    def work(i):
        coef_i = [coef[at, i] for at in range(6)]
        for c in range(comps):
            mid, total = gathered_sum(beside, src, c, i, coef_i)
            if scale is not None:
                term = scale[i] * mid
                right[c, i] = term
            else:
                term = right[c, i]
            dst[c, i] = (total + term) + (1.0 - WEIGHT) * mid

    over_layers(low, high, step, work)


def residual(beside, src, coef, right, back, c, i, coef_i):
    mid, total = gathered_sum(beside, src, c, i, coef_i)
    return ((total + right[c, i]) - WEIGHT * mid) * back[i]


def from_zero(rhs, scale, right, dst, comps, low, high, step=2):
    def work(i):
        for c in range(comps):
            term = scale[i] * rhs[c, i]
            right[c, i] = term
            dst[c, i] = term

    over_layers(low, high, step, work)


def split_rows(lane):
    return lane // 64, (lane & 63) // 32, lane & 31


def matrix_0_1(factor, transposed=False):
    shape = (LANES, 2 * LANES) if transposed else (2 * LANES, LANES)
    fine, coarse = iota(shape, 1 if transposed else 0), iota(shape, 0 if transposed else 1)
    lane = fine & (LANES - 1)
    goal = (fine // LANES) * 64 + (lane // 64) * 32 + (lane & 63) // 2
    return jnp.where(goal == coarse, factor, 0.0).astype(jnp.bfloat16)


def matrix_1_2(field, factor, transposed=False):
    shape = (LANES, LANES)
    fine, coarse = iota(shape, 1 if transposed else 0), iota(shape, 0 if transposed else 1)
    goal = field * 32 + ((fine & 63) // 32) * 16 + (fine & 31) // 2
    return jnp.where(goal == coarse, factor, 0.0).astype(jnp.bfloat16)


def times(value, matrix):
    total = None
    for _ in range(3):
        part = value.astype(jnp.bfloat16)
        value = value - part.astype(F32)
        term = jnp.dot(part, matrix, preferred_element_type=F32)
        total = term if total is None else total + term
    return total


def pair_y(value):
    first = value[:MID] + value[MID : 2 * MID]
    second = value[2 * MID : 3 * MID] + value[3 * MID :]
    return first, second


def vmem(*shape):
    return pltpu.VMEM((*shape, LANES), F32)


def shaped(*dims):
    return jax.ShapeDtypeStruct((*dims, LANES), F32)


def start(copies):
    for copy in copies:
        copy.start()
    return copies


def finish(copies):
    for copy in copies:
        copy.wait()


def place_in_mesh():
    group, member = lax.axis_index("grp"), lax.axis_index("dev")
    return group, member, group * lax.axis_size("dev") + member


def slot_for(source, base, blocks, dst, owner):
    slot = 0
    for j in range(blocks):
        slot = jnp.where(lax.div(source[base + dst * blocks + j] - base, blocks) == owner, j, slot)
    return slot


def pick(viscosity, velocity, block, fields):
    parts, at = [], 0
    if fields[0] is None:
        parts.append((pl.ds(0, 1), viscosity.at[pl.ds(block, 1)]))
        fields, at = fields[1:], 1
    if fields:
        parts.append((pl.ds(at, len(fields)), velocity.at[block, pl.ds(fields[0], len(fields))]))
    return parts


def load_kernel(*refs):
    count = (len(refs) - 1) // 2
    copies = [
        pltpu.make_async_copy(array, out, refs[-1].at[n]) for n, (array, out) in enumerate(zip(refs[:count], refs[count:-1]))
    ]
    finish(start(copies))


def load(*arrays):
    arrays = [pltpu.with_memory_space_constraint(array, pltpu.HBM) for array in arrays]
    return pl.pallas_call(
        load_kernel,
        in_specs=[ANY] * len(arrays),
        out_specs=[WHOLE] * len(arrays),
        out_shape=[jax.ShapeDtypeStruct(array.shape, array.dtype) for array in arrays],
        scratch_shapes=[pltpu.SemaphoreType.DMA((len(arrays),))],
        compiler_params=pltpu.CompilerParams(vmem_limit_bytes=16 * MEGA),
        name="load",
    )(*arrays)


def pack_kernel(members, fields, sends, source, *refs):
    raw, outs = refs[: -len(sends)], refs[-len(sends) :]
    blocks = raw[0].shape[0]
    group, member, _ = place_in_mesh()
    base = group * members * blocks
    for out, (turn, owners) in zip(outs, sends):
        for at, n in enumerate(owners):
            slot = slot_for(source, base, blocks, member ^ turn, member ^ n)
            for f, field in enumerate(fields):
                out[at, f] = raw[2 * n][slot] if field is None else raw[2 * n + 1][slot, field]


def pack(source, raw, fields, members, sends):
    edge, flat = raw[0].shape[-2:]
    return pl.pallas_call(
        functools.partial(pack_kernel, members, fields, sends),
        in_specs=[SCALARS] + [WHOLE] * len(raw),
        out_specs=[WHOLE] * len(sends),
        out_shape=[jax.ShapeDtypeStruct((len(owners), len(fields), edge, flat), F32) for _, owners in sends],
        compiler_params=pltpu.CompilerParams(vmem_limit_bytes=16 * MEGA),
        name="pack",
    )(source, *raw)


def assemble_kernel(members, fields, sends, source, viscosity, velocity, viscosity_other, velocity_other, *refs):
    received, (own, facing, outer, tall, turned, sems) = refs[: len(sends)], refs[len(sends) :]
    blocks = viscosity.shape[0]
    edge = own.shape[1]
    group, member, _ = place_in_mesh()
    base = group * members * blocks

    def each_copy(act):
        for j in range(blocks):
            owner = lax.div(source[base + member * blocks + j] - base, blocks)
            rows = pl.ds((j % 2) * 64 + (j // 2) * edge, edge)
            for n, arrays in enumerate(((viscosity, velocity), (viscosity_other, velocity_other))):

                @pl.when(owner == member ^ n)
                def _(arrays=arrays):
                    for f, (goal, part) in enumerate(pick(*arrays, j, fields)):
                        act(pltpu.make_async_copy(part, tall.at[goal, rows], sems.at[j, f]))

            for part, (turn, owners) in zip(received, sends):
                for at, n in enumerate(owners):

                    @pl.when(owner == member ^ turn ^ n)
                    def _(part=part, at=at):
                        act(pltpu.make_async_copy(part.at[at], tall.at[:, rows], sems.at[j, 0]))

    each_copy(lambda copy: copy.start())
    each_copy(lambda copy: copy.wait())
    for f in range(len(fields)):
        for at in range(edge * edge // LANES):
            turned[f, pl.ds(at * LANES, LANES)] = tall[f, :, pl.ds(at * LANES, LANES)].T
        for i in range(edge):
            for lo in range(4):
                rows = pl.ds(lo * MID, MID)
                own[f, i, rows] = turned[f, pl.ds(lo * edge + i, MID, 4 * edge)]
    odd = (member & 1) == 1
    for goal, low in ((facing, jnp.where(odd, 0, edge - HALO)), (outer, jnp.where(odd, edge - HALO, 0))):
        for f in range(len(fields)):
            for i in range(HALO):
                goal[f, i] = own[f, low + i]


def assemble(source, raw, fields, received, members, sends):
    _, width, edge, flat = received[0].shape
    rows = flat // edge
    return pl.pallas_call(
        functools.partial(assemble_kernel, members, fields, sends),
        in_specs=[SCALARS] + [WHOLE] * (4 + len(sends)),
        out_specs=[WHOLE] * 3,
        scratch_shapes=[
            pltpu.VMEM((width, LANES, flat), F32),
            vmem(width, flat),
            pltpu.SemaphoreType.DMA((raw[0].shape[0], 2)),
        ],
        out_shape=[shaped(width, layers, rows) for layers in (edge, HALO, HALO)],
        compiler_params=pltpu.CompilerParams(vmem_limit_bytes=16 * MEGA),
        name="assemble",
    )(source, *raw, *received)


def copy_layers(target, first, source, at, count):
    def work(i):
        target[first + i] = source[at, i]

    over_layers(0, count, 4 if count % 4 == 0 else count, work)


def copy_halos(target, near, beyond, at, width, me):
    odd = (me & 1) == 1
    low, high = BASE0 - HALO, BASE0 + width
    copy_layers(target, jnp.where(odd, low, high), near, at, HALO)
    copy_layers(target, jnp.where(odd, high, low), beyond, at, HALO)


def viscosity_kernel(total_x, own, near, beyond, coef, scale, back, coef1, scale1, back1, nu2, nu, nu1, sums):
    width = own.shape[1]
    layers, layers1 = width + 2 * BASE0, width // 2 + 2 * BASE1
    _, _, me = place_in_mesh()
    copy_layers(nu, BASE0, own, 0, width)
    copy_halos(nu, near, beyond, 0, width, me)
    make_weights(0, beside0, nu, coef, scale, back, 2, layers - 2, me * width - BASE0, total_x, step=8)

    def nu_sums(t):
        a, b = pair_y(nu[2 + 2 * t] + nu[3 + 2 * t])
        sums[t, :, pl.ds(0, LANES)] = a
        sums[t, :, pl.ds(LANES, LANES)] = b

    count = layers1 - 2
    over_layers(0, count, count // 2, nu_sums)
    value = times(sums[...].reshape(count * MID, 2 * LANES), matrix_0_1(0.125))
    nu1[pl.ds(1, count)] = value.reshape(count, MID, LANES)
    make_weights(
        1, beside1, nu1, coef1, scale1, back1, 2, layers1 - 2, me * (width // 2) - BASE1, total_x // 2, step=8
    )
    mine = width // 4
    paired = [nu1[BASE1 + 2 * t] + nu1[BASE1 + 2 * t + 1] for t in range(mine)]
    value = times(jnp.concatenate(paired, axis=0), matrix_1_2(3, 0.125))
    nu2[...] = value.reshape(mine, MID, LANES)


def viscosity_weights(arrays, total_x):
    width, rows = arrays[0].shape[1:3]
    layers, layers1 = width + 2 * BASE0, width // 2 + 2 * BASE1
    return pl.pallas_call(
        functools.partial(viscosity_kernel, total_x),
        in_specs=[WHOLE] * 3,
        out_specs=[WHOLE] * 7,
        out_shape=[
            shaped(6, layers, rows), shaped(layers, rows), shaped(layers, rows),
            shaped(6, layers1, MID), shaped(layers1, MID), shaped(layers1, MID),
            shaped(width // 4, MID),
        ],
        scratch_shapes=[
            vmem(layers, rows), vmem(layers1, MID), pltpu.VMEM((layers1 - 2, MID, 2 * LANES), F32),
        ],
        compiler_params=pltpu.CompilerParams(vmem_limit_bytes=24 * MEGA),
        cost_estimate=pl.CostEstimate(flops=200_000_000, bytes_accessed=8_000_000, transcendentals=0),
        name="viscosity",
    )(*arrays)


def down_kernel(
    comp_at, first_field, own, near, beyond, coef, scale, back, coef1, scale1, back1, *refs,
):
    before, (A, right, B1, right1, message, B, sums, rhs1, A1) = refs[0], refs[1:]
    comps = len(comp_at)
    width = own.shape[1]
    layers, layers1 = width + 2 * BASE0, width // 2 + 2 * BASE1
    _, _, me = place_in_mesh()
    for c, at in enumerate(comp_at):
        copy_layers(A.at[c], BASE0, own, at, width)
        copy_halos(A.at[c], near, beyond, at, width, me)
    sweep(beside0, A, B, coef, right, comps, 2, layers - 2, scale=scale, step=11)
    sweep(beside0, B, A, coef, right, comps, 3, layers - 3, step=14)
    count = layers1 - 4

    def residual_sums(t):
        found = [None] * comps
        for d in range(2):
            i = 4 + 2 * t + d
            coef_i = [coef[at, i] for at in range(6)]
            for c in range(comps):
                value = residual(beside0, A, coef, right, back, c, i, coef_i)
                found[c] = value if d == 0 else found[c] + value
        for c in range(comps):
            a, b = pair_y(found[c])
            sums[c, t, :, pl.ds(0, LANES)] = a
            sums[c, t, :, pl.ds(LANES, LANES)] = b

    over_layers(0, count, 5, residual_sums)
    matrix = matrix_0_1(0.125)
    for c in range(comps):
        value = times(sums[c].reshape(count * MID, 2 * LANES), matrix)
        rhs1[c, pl.ds(2, count)] = value.reshape(count, MID, LANES)

    from_zero(rhs1, scale1, right1, A1, comps, 2, layers1 - 2, step=8)
    sweep(beside1, A1, B1, coef1, right1, comps, 3, layers1 - 3, step=11)
    mine = width // 4
    chained = before.shape[0] > mine
    total = before[pl.ds(EDGES if chained else 0, mine)].reshape(mine * MID, LANES)
    paired = [[] for _ in range(comps)]
    for t in range(mine):
        found = [None] * comps
        for d in range(2):
            i = BASE1 + 2 * t + d
            coef_i = [coef1[at, i] for at in range(6)]
            for c in range(comps):
                value = residual(beside1, B1, coef1, right1, back1, c, i, coef_i)
                found[c] = value if d == 0 else found[c] + value
        for c in range(comps):
            paired[c].append(found[c])
    for c in range(comps):
        total = total + times(jnp.concatenate(paired[c], axis=0), matrix_1_2(first_field + c, 0.125))
    message[pl.ds(EDGES, mine)] = total.reshape(mine, MID, LANES)

    first, last = BASE1 + 1, BASE1 + width // 2 - SIDE1
    odd = (me & 1) == 1
    for low, at in ((jnp.where(odd, first, last), 0), (jnp.where(odd, last, first), EDGES + mine)):
        if chained:
            message[pl.ds(at, EDGES)] = before[pl.ds(at, EDGES)]
        for c in range(comps):
            for t in range(FETCHED):
                message[at + (first_field + c) * FETCHED + t] = B1[c, low + t]


def down(arrays, comp_at, first_field, weights, before):
    width, rows = arrays[0].shape[1:3]
    comps = len(comp_at)
    layers, layers1, mine = width + 2 * BASE0, width // 2 + 2 * BASE1, width // 4
    return pl.pallas_call(
        functools.partial(down_kernel, comp_at, first_field),
        in_specs=[WHOLE] * 10,
        out_specs=[WHOLE] * 5,
        out_shape=[
            shaped(comps, layers, rows), shaped(comps, layers, rows),
            shaped(comps, layers1, MID), shaped(comps, layers1, MID),
            shaped(mine + 2 * EDGES, MID),
        ],
        scratch_shapes=[
            vmem(comps, layers, rows),
            pltpu.VMEM((comps, layers1 - 4, MID, 2 * LANES), F32),
            vmem(comps, layers1, MID), vmem(comps, layers1, MID),
        ],
        compiler_params=pltpu.CompilerParams(vmem_limit_bytes=24 * MEGA),
        cost_estimate=pl.CostEstimate(flops=200_000_000, bytes_accessed=8_000_000, transcendentals=0),
        name="down",
    )(*arrays, *weights, before)


def up_kernel(total_x, parts, *refs):
    (message, beside, beyond, far, other), refs = refs[:5], refs[5:]
    coef, coef1, refs = refs[0], refs[1], refs[2:]
    comps = []
    for part in parts:
        comps += [(*refs[:4], n) for n in range(part)]
        refs = refs[4:]
    out = refs[0]
    (
        A, B, refined, turned, blocks, A1, B1, refined1,
        window, A2, B2, nu2, coef2, scale2, back2, right2, A3, B3, nu3, coef3, scale3, right3, rhs3,
        out_sems,
    ) = refs[1:]
    width = blocks.shape[2]
    mine = width // 4
    _, _, me = place_in_mesh()

    layers2 = (2 * REACH + 1) * mine + 2
    own2 = 1 + REACH * mine
    first2 = me * mine - own2
    lane = iota((MID, LANES), 1)
    zeros = jnp.zeros((MID, LANES), F32)
    nu2[0] = zeros
    nu2[layers2 - 1] = zeros
    odd = (me & 1) == 1
    side = jnp.where(odd, -1, 1)
    theirs = mine + EDGES
    pieces = [(message, EDGES, 0), (beside, EDGES, side), (beyond, 0, -side), (beyond, theirs, -2 * side)]
    pieces += [(far, EDGES, -3 * side), (other, 0, 2 * side), (other, theirs, 3 * side)]
    for piece, at, place_of in pieces:
        goal = own2 + place_of * mine
        for i in range(mine):
            value = piece[at + i]
            window[goal + i] = value
            value = jnp.where(lane >= 96, value, 0.0)
            value = value + spin(value, 32, 1)
            nu2[goal + i] = value + spin(value, 64, 1)
    reach3 = 9
    low2, high2 = own2 - 2 * reach3 - 2, own2 + mine + 2 * reach3 + 2
    make_weights(2, beside2, nu2, coef2, scale2, back2, low2, high2, first2, total_x // 4, step=16)

    def zero2(i):
        term = scale2[i] * window[i]
        right2[0, i] = term
        A2[0, i] = term

    over_layers(low2, high2, 16, zero2)
    sweep(beside2, A2, B2, coef2, right2, 1, low2 + 1, high2 - 1, step=23)

    own3 = reach3 + 2
    mine3 = mine // 2
    row = iota((MID, LANES), 0)

    def both(value):
        value = value + jnp.where((row & 1) == 0, spin(value, -1, 0), spin(value, 1, 0))
        return (value + jnp.where((lane & 1) == 0, spin(value, -1, 1), spin(value, 1, 1))) * 0.125

    def nu_down(t):
        nu3[1 + t] = both(nu2[low2 + 2 * t] + nu2[low2 + 2 * t + 1])

    def rhs_down(t):
        total = None
        for d in range(2):
            i = low2 + 2 + 2 * t + d
            value = residual(beside2, B2, coef2, right2, back2, 0, i, [coef2[at, i] for at in range(6)])
            total = value if total is None else total + value
        rhs3[0, 2 + t] = both(total)

    over_layers(0, mine3 + 2 * reach3 + 2, 24, nu_down)
    over_layers(0, mine3 + 2 * reach3, 11, rhs_down)
    low3, high3 = own3 - reach3, own3 + mine3 + reach3
    make_weights(
        3, beside3, nu3, coef3, scale3, None, low3, high3, me * mine3 - own3, total_x // 8, step=high3 - low3
    )
    from_zero(rhs3, scale3, right3, A3, 1, low3, high3, step=high3 - low3)
    src, dst = A3, B3
    for turn in range(1, BOTTOM):
        low, high = low3 + turn, high3 - turn
        sweep(beside3, src, dst, coef3, right3, 1, low, high, step=high - low)
        src, dst = dst, src
    e3 = src

    for t in range(mine3 + 4):
        value = e3[0, own3 - 2 + t]
        for d in range(2):
            i = own2 - 4 + 2 * t + d
            A2[0, i] = B2[0, i] + value
    low, high = own2 - 3, own2 + mine + 3
    sweep(beside2, A2, B2, coef2, right2, 1, low, high, step=high - low)
    sweep(beside2, B2, A2, coef2, right2, 1, low + 1, high - 1, step=high - low - 2)

    count = mine + 4
    value = A2[0, pl.ds(own2 - 2, count)].reshape(count * MID, LANES)
    matrix = jnp.concatenate([matrix_1_2(c, 1.0, transposed=True) for c in range(3)], axis=1)
    refined1[...] = times(value, matrix).reshape(count, MID, 3 * LANES)
    low, high = BASE1 - SIDE1, BASE1 + width // 2 + SIDE1
    for t in range(count):
        for d in range(2):
            i = BASE1 - 4 + 2 * t + d
            if not low <= i < high:
                continue
            for c, (_, _, u1, _, n) in enumerate(comps):
                before, after = i - low, i - (high - FETCHED)
                if before < FETCHED or after >= 0:
                    edge = c * FETCHED + (before if before < FETCHED else after)
                    near, past = beside[edge], beyond[mine + edge]
                    value = jnp.where(odd, near, past) if before < FETCHED else jnp.where(odd, past, near)
                else:
                    value = u1[n, i]
                A1[c, i] = value + refined1[t, :, pl.ds(c * LANES, LANES)]
    rights1 = [(b1, n) for _, _, _, b1, n in comps]
    sweep_many(beside1, A1, B1, coef1, rights1, low + 1, high - 1, 0, 10)
    sweep_many(beside1, B1, A1, coef1, rights1, low + 2, high - 2, 0, 9)

    layers = width + 2 * SIDE0
    shift = BASE0 - SIDE0
    count = layers // 2
    matrix = matrix_0_1(1.0, transposed=True)
    for c in range(3):
        value = A1[c, pl.ds(BASE1 - SIDE0 // 2, count)].reshape(count * MID, LANES)
        refined[c] = times(value, matrix).reshape(count, MID, 2 * LANES)

    def add(t):
        for c, (u0, _, _, _, n) in enumerate(comps):
            a, b = refined[c, t, :, pl.ds(0, LANES)], refined[c, t, :, pl.ds(LANES, LANES)]
            value = jnp.concatenate([a, a, b, b], axis=0)
            for d in range(2):
                A[c, 2 * t + d] = u0[n, 2 * t + d + shift] + value

    over_layers(0, count, 6, add)
    rights = [(b0, n) for _, b0, _, _, n in comps]
    sweep_many(beside0, A, B, coef, rights, 1, layers - 1, shift, 8)
    sweep_many(beside0, B, A, coef, rights, SIDE0, layers - SIDE0, shift, 8)

    writes = []
    for c in range(3):
        for i in range(width):
            for lo in range(4):
                turned[c, pl.ds(lo * width + i, MID, 4 * width)] = A[c, SIDE0 + i, pl.ds(lo * MID, MID)]
        for at in range(width * width // LANES):
            tall = turned[c, pl.ds(at * LANES, LANES)].T
            for slot in range(4):
                first_row = (slot % 2) * 64 + (slot // 2) * width
                blocks[slot, c, :, pl.ds(at * LANES, LANES)] = tall[first_row : first_row + width]
        writes += start([pltpu.make_async_copy(blocks.at[:, c], out.at[:, c], out_sems.at[c])])
    finish(writes)


def sweep_many(beside, src, dst, coef, rights, low, high, shift, step):
    def work(i):
        coef_i = [coef[at, i + shift] for at in range(6)]
        for c, (right, n) in enumerate(rights):
            mid, total = gathered_sum(beside, src, c, i, coef_i)
            dst[c, i] = (total + right[n, i + shift]) + (1.0 - WEIGHT) * mid

    over_layers(low, high, step, work)


def up(pieces, weights, chunks, parts, width, total_x):
    rows = weights[0].shape[2]
    layers, layers1, mine = width + 2 * SIDE0, width // 2 + 2 * BASE1, width // 4
    layers2, layers3 = (2 * REACH + 1) * mine + 2, mine // 2 + 22
    out_shape = (4, 3, width, width * rows)
    operands = [*pieces, *weights]
    for chunk in chunks:
        operands += chunk
    return pl.pallas_call(
        functools.partial(up_kernel, total_x, parts),
        in_specs=[WHOLE] * len(operands),
        out_specs=ANY,
        out_shape=jax.ShapeDtypeStruct(out_shape, F32),
        scratch_shapes=[
            vmem(3, layers, rows), vmem(3, layers, rows),
            pltpu.VMEM((3, layers // 2, MID, 2 * LANES), F32), vmem(3, width * rows), pltpu.VMEM(out_shape, F32),
            vmem(3, layers1, MID), vmem(3, layers1, MID),
            pltpu.VMEM((mine + 4, MID, 3 * LANES), F32),
            vmem(layers2, MID), vmem(1, layers2, MID), vmem(1, layers2, MID), vmem(layers2, MID),
            vmem(6, layers2, MID), vmem(layers2, MID), vmem(layers2, MID), vmem(1, layers2, MID),
            vmem(1, layers3, MID), vmem(1, layers3, MID), vmem(layers3, MID),
            vmem(6, layers3, MID), vmem(layers3, MID), vmem(1, layers3, MID), vmem(1, layers3, MID),
            pltpu.SemaphoreType.DMA((3,)),
        ],
        compiler_params=pltpu.CompilerParams(vmem_limit_bytes=32 * MEGA),
        cost_estimate=pl.CostEstimate(flops=400_000_000, bytes_accessed=16_000_000, transcendentals=0),
        name="up",
    )(*operands)


def local(velocity_old, viscosity_old, source):
    axes = ("grp", "dev")
    members = lax.axis_size("dev")
    count = lax.axis_size("grp") * members
    edge = velocity_old.shape[2]
    total_x = count * edge
    turns = turn_order(members)
    pairs = [(m, m ^ 1) for m in range(members)]
    own_raw = load(viscosity_old, velocity_old)
    raw = (*own_raw, *(lax.ppermute(array, "dev", pairs) for array in (viscosity_old, velocity_old)))
    source = pltpu.with_memory_space_constraint(source, pltpu.HBM)

    chunks = ((None, 0), (1, 2))
    late = tuple((turn, (0, 1)) for turn in turns)
    early = ((turns[0], (0,)),)
    plans = (early + ((turns[0], (1,)),) + late[1:], late)
    received = []
    for fields, plan in zip(chunks, plans):
        packed = []
        if plan[0] in early:
            packed += pack(source, own_raw, fields, members, early)
        packed += pack(source, raw, fields, members, plan[len(packed) :])
        received.append(
            [lax.ppermute(sent, "dev", [(m, m ^ turn) for m in range(members)]) for (turn, _), sent in zip(plan, packed)]
        )

    def swap(array, hop):
        return lax.ppermute(array, axes, [(i, i ^ hop) for i in range(count)])

    def swap_outward(array, hop):
        goals = [(i, i + hop if i & hop else i - hop) for i in range(count)]
        return lax.ppermute(array, axes, [(i, to) for i, to in goals if 0 <= to < count])

    grids = []
    for fields, plan, slots in zip(chunks, plans, received):
        grid, facing, outer = assemble(source, raw, fields, slots, members, plan)
        beyond = swap_outward(outer, 1)
        grids.append((grid, swap(facing, 1), beyond))
    *weights, sent = viscosity_weights(grids[0], total_x)
    kept = []
    for fields, arrays in zip(chunks, grids):
        comps = [(at, field) for at, field in enumerate(fields) if field is not None]
        *state, sent = down(arrays, tuple(at for at, _ in comps), comps[0][1], weights, sent)
        kept.append(state)

    beside = swap(sent, 1)
    hops = [(i, i - 3 + 6 * (i % 2)) for i in range(count)]
    far = lax.ppermute(sent, axes, [(i, to) for i, to in hops if 0 <= to < count])
    mine = edge // 4
    beyond = swap_outward(jnp.concatenate([sent[EDGES:], beside[EDGES : EDGES + mine]], axis=0), 1)
    came, far = lax.optimization_barrier((beyond, far))
    other = swap(came, 1)
    widths = tuple(state[0].shape[0] for state in kept)
    return up((sent, beside, beyond, far, other), (weights[0], weights[3]), kept, widths, edge, total_x)


def turn_order(members):
    if members & (members - 1):
        raise ValueError("members")
    return tuple(range(members - 2, 0, -2))


def solution(mesh):
    return jax.shard_map(
        local,
        mesh=mesh,
        in_specs=(P(("grp", "dev"), None, None, None), P(("grp", "dev"), None, None), P()),
        out_specs=P(("grp", "dev"), None, None, None),
        check_vma=False,
    )
```

time: 871 us -> 94.9 us (0.11)
  local copies, waits for them, and re-layouts: 466 us -> 0.01 us
  other arithmetic: 126 us -> 0.01 us
  starting transfers between devices: 144 us -> 19.5 us
  waiting for transfers between devices: 103 us -> 45.9 us
  Pallas kernels: 0 us -> 28.2 us
  between operations: 15.6 us -> 0.31 us
    reshape x10 -> x0, local copies, waits for them, and re-layouts: 349 us -> none  [the longest x3 172 us: coarsen(): grid.reshape(channels, length // 2, 2, width_y // 2, 2, width_y // 2, 2)]
    ppermute x54 -> x17, starting transfers between devices: 144 us -> 19.5 us  [the longest x3 10.1 us: swap_outward(): lax.ppermute(array, axes, [(i, to) for i, to in goals if 0 <= to < count])]
    reduce_sum x6 -> x0, other arithmetic: 58.2 us -> none  [coarsen(): shaped.mean(axis=(2, 4, 6)).reshape(channels, length // 2, plane // 4)]
    broadcast_in_dim x9 -> x0, local copies, waits for them, and re-layouts: 44.5 us -> none  [the longest x6 44.5 us: refine(): jnp.broadcast_to(shaped, (channels, length, 2, width_y, 2, width_y, 2))]
    all_gather x2 -> x0, waiting for transfers between devices: 37.8 us -> none  [the longest x1 27.3 us: local(): lax.all_gather(viscosity_old, 'dev', axis=0, tiled=True)]
    pallas_call x0 -> x10, Pallas kernels: none -> 28.2 us  [the longest x1 9.89 us: up(): pl.pallas_call(functools.partial(up_kernel, total_x, parts), in_specs=[WH...]
    gather x5 -> x0, local copies, waits for them, and re-layouts: 24.1 us -> none  [the longest x3 19.3 us: local(): jnp.take(pieces[0], clipped, axis=0)]
    another operation x4 -> x0, local copies, waits for them, and re-layouts: 23.7 us -> none  [the longest x1 21.9 us: coarsen(): grid.reshape(channels, length // 2, 2, width_y // 2, 2, width_y // 2, 2)]
  transfers between devices with their start and end apart: 56 -> 17, of which waited for: 20 -> 10; matrix products, arithmetic and copies ran while one was open for 41% -> 0% of each run, Pallas kernels for 0% -> 14%
where the time goes in v1:
time: 94.9 us; the launch traced here: 94 us
  waiting for transfers between devices  45.9 us (48%)
  Pallas kernels  28.2 us (30%)
  starting transfers between devices  19.5 us (21%)
    ppermute x7, waiting for transfers between devices, local(): lax.ppermute(sent, 'dev', [(m, m ^ turn) for m in range(members)])  37.1 us
    ppermute x3, starting transfers between devices, swap_outward(): lax.ppermute(array, axes, [(i, to) for i, to in goals if 0 <= to < count])  10.1 us
    pallas_call x1, Pallas kernels, up(): pl.pallas_call(functools.partial(up_kernel, total_x, parts), in_specs=[WH...  9.89 us
    pallas_call x2, Pallas kernels, down(): pl.pallas_call(functools.partial(down_kernel, comp_at, first_field), in_s...  7.75 us
    pallas_call x2, Pallas kernels, assemble(): pl.pallas_call(functools.partial(assemble_kernel, members, fields, sends)...  4.51 us
    ppermute x7, starting transfers between devices, local(): lax.ppermute(sent, 'dev', [(m, m ^ turn) for m in range(members)])  4.09 us
    ppermute x1, waiting for transfers between devices, local(): lax.ppermute(sent, axes, [(i, to) for i, to in hops if 0 <= to < count])  3.83 us
    ppermute x1, starting transfers between devices, local(): lax.ppermute(sent, axes, [(i, to) for i, to in hops if 0 <= to < count])  2.82 us
  transfers between devices with their start and end apart: 17, of which 10 were waited for; matrix products, arithmetic and copies ran while one was open for 0% of the time, Pallas kernels for 14%

profile of v1, /device:TPU:7, one launch (start us, length us, event | category | flops | bytes accessed | tf_op | source)
XLA Modules:
  0.0 94.0 jit_solution(13354130893694970079)
XLA Ops:
  0.0 0.7 collective-permute-start.1
  0.7 1.6 %load.1 = (f32[4,32,1024]{2,1,0:T(8,128)S(1)}, f32[4,3,32,1024]{3,2,1,0:T(8,128)S(1)}) custom-call(f32[4,32,1024]{2,1,0:T(8,128)} %refs_0_.1, f32[4,3,32,1024]{3,2,1,0:T(8,128)} %refs_1_.1), custom_call_target="tpu_custom_call" | custom-call | tf_op jit(solution)/shard_map/load/pallas_call | solution.py:258
  2.3 0.7 pack.4
  3.1 1.6 %collective-permute-done.refs_2_.viscosity_other = f32[4,32,1024]{2,1,0:T(8,128)S(1)} collective-permute-done((f32[4,32,1024]{2,1,0:T(8,128)}, f32[4,32,1024]{2,1,0:T(8,128)S(1)}, u32[]{:S(2)}, u32[]{:S(2)}) %collective-permute-start) | collective-permute-done | bytes 524320 | tf_op jit(solution)/shard_map/ppermute | solution.py:698
  4.7 0.8 pack.5
  5.5 0.8 collective-permute-start.8
  6.3 0.7 collective-permute-start.9
  7.0 1.2 %collective-permute-start.10 = (f32[2,2,32,1024]{3,2,1,0:T(8,128)S(1)}, f32[2,2,32,1024]{3,2,1,0:T(8,128)S(1)}, u32[]{:S(2)}, u32[]{:S(2)}) collective-permute-start(f32[2,2,32,1024]{3,2,1,0:T(8,128)S(1)} %get-tuple-element.48), channel_id=1, source_target_pairs={{0,2},{1,3},{2,0},{3,1},{4,6},{5,7},{6,4},{7,5},{8,10},{9,11},{10,... | collective-permute-start | bytes 1572872 | tf_op jit(solution)/shard_map/ppermute | solution.py:712
  8.2 0.8 pack.3
  9.0 0.8 collective-permute-start.2
  9.8 1.6 %collective-permute-done.7.refs_0_ = f32[1,2,32,1024]{3,2,1,0:T(8,128)S(1)} collective-permute-done((f32[1,2,32,1024]{3,2,1,0:T(8,128)S(1)}, f32[1,2,32,1024]{3,2,1,0:T(8,128)S(1)}, u32[]{:S(2)}, u32[]{:S(2)}) %collective-permute-start.7) | collective-permute-done | bytes 262176 | tf_op jit(solution)/shard_map/ppermute | solution.py:712
  11.6 5.4 %collective-permute-done.8.refs_1_ = f32[1,2,32,1024]{3,2,1,0:T(8,128)S(1)} collective-permute-done((f32[1,2,32,1024]{3,2,1,0:T(8,128)S(1)}, f32[1,2,32,1024]{3,2,1,0:T(8,128)S(1)}, u32[]{:S(2)}, u32[]{:S(2)}) %collective-permute-start.8) | collective-permute-done | bytes 262176 | tf_op jit(solution)/shard_map/ppermute | solution.py:712
  17.0 0.3 collective-permute-start.4
  17.2 12.6 %collective-permute-done.9.refs_2_ = f32[2,2,32,1024]{3,2,1,0:T(8,128)S(1)} collective-permute-done((f32[2,2,32,1024]{3,2,1,0:T(8,128)S(1)}, f32[2,2,32,1024]{3,2,1,0:T(8,128)S(1)}, u32[]{:S(2)}, u32[]{:S(2)}) %collective-permute-start.9) | collective-permute-done | bytes 524320 | tf_op jit(solution)/shard_map/ppermute | solution.py:712
  29.9 2.4 %assemble.3 = (f32[2,32,32,128]{3,2,1,0:T(8,128)S(1)}, f32[2,7,32,128]{3,2,1,0:T(8,128)S(1)}, f32[2,7,32,128]{3,2,1,0:T(8,128)S(1)}) custom-call(s32[128]{0:T(128)} %source.9, f32[4,32,1024]{2,1,0:T(8,128)S(1)} %get-tuple-element.38.refs_0_.viscosity, f32[4,3,32,1024]{3,2,1,0:T(8,128)S(1)} %get-tuple-element.39.refs_1_.velocity, ...), custom_call_target="tpu_custom_call" | custom-call | tf_op jit(solution)/shard_map/assemble/pallas_call | solution.py:337
  32.3 1.1 %collective-permute-start.11 = (f32[2,7,32,128]{3,2,1,0:T(8,128)S(1)}, f32[2,7,32,128]{3,2,1,0:T(8,128)S(1)}, u32[]{:S(2)}, u32[]{:S(2)}) collective-permute-start(f32[2,7,32,128]{3,2,1,0:T(8,128)S(1)} %get-tuple-element.50), channel_id=1, source_target_pairs={{0,1},{1,0},{2,3},{3,2},{4,5},{5,4},{6,7},{7,6},{8,9},{9,8},{10,11... | collective-permute-start | bytes 688136 | tf_op jit(solution)/shard_map/ppermute | solution.py:716
  33.4 3.0 %collective-permute-start.12 = (f32[2,7,32,128]{3,2,1,0:T(8,128)S(1)}, f32[2,7,32,128]{3,2,1,0:T(8,128)S(1)}, u32[]{:S(2)}, u32[]{:S(2)}) collective-permute-start(f32[2,7,32,128]{3,2,1,0:T(8,128)S(1)} %get-tuple-element.51), channel_id=1, source_target_pairs={{1,2},{2,1},{3,4},{4,3},{5,6},{6,5},{7,8},{8,7},{9,10},{10,9},{11,... | collective-permute-start | bytes 688136 | tf_op jit(solution)/shard_map/ppermute | solution.py:720
  36.4 3.0 %collective-permute-done.2.refs_0_ = f32[2,2,32,1024]{3,2,1,0:T(8,128)S(1)} collective-permute-done((f32[2,2,32,1024]{3,2,1,0:T(8,128)S(1)}, f32[2,2,32,1024]{3,2,1,0:T(8,128)S(1)}, u32[]{:S(2)}, u32[]{:S(2)}) %collective-permute-start.2) | collective-permute-done | bytes 524320 | tf_op jit(solution)/shard_map/ppermute | solution.py:712
  39.5 14.5 %collective-permute-done.3.refs_1_ = f32[2,2,32,1024]{3,2,1,0:T(8,128)S(1)} collective-permute-done((f32[2,2,32,1024]{3,2,1,0:T(8,128)S(1)}, f32[2,2,32,1024]{3,2,1,0:T(8,128)S(1)}, u32[]{:S(2)}, u32[]{:S(2)}) %collective-permute-start.3) | collective-permute-done | bytes 524320 | tf_op jit(solution)/shard_map/ppermute | solution.py:712
  54.0 2.1 %assemble.2 = (f32[2,32,32,128]{3,2,1,0:T(8,128)S(1)}, f32[2,7,32,128]{3,2,1,0:T(8,128)S(1)}, f32[2,7,32,128]{3,2,1,0:T(8,128)S(1)}) custom-call(s32[128]{0:T(128)} %source.9, f32[4,32,1024]{2,1,0:T(8,128)S(1)} %get-tuple-element.38.refs_0_.viscosity, f32[4,3,32,1024]{3,2,1,0:T(8,128)S(1)} %get-tuple-element.39.refs_1_.velocity, ...), custom_call_target="tpu_custom_call" | custom-call | tf_op jit(solution)/shard_map/assemble/pallas_call | solution.py:337
  56.1 0.6 collective-permute-start.5
  56.6 3.1 %collective-permute-start.6 = (f32[2,7,32,128]{3,2,1,0:T(8,128)S(1)}, f32[2,7,32,128]{3,2,1,0:T(8,128)S(1)}, u32[]{:S(2)}, u32[]{:S(2)}) collective-permute-start(f32[2,7,32,128]{3,2,1,0:T(8,128)S(1)} %get-tuple-element.45), channel_id=1, source_target_pairs={{1,2},{2,1},{3,4},{4,3},{5,6},{6,5},{7,8},{8,7},{9,10},{10,9},{11,... | collective-permute-start | bytes 688136 | tf_op jit(solution)/shard_map/ppermute | solution.py:720
  59.8 2.2 %viscosity.1 = (f32[6,48,32,128]{3,2,1,0:T(8,128)S(1)}, f32[48,32,128]{2,1,0:T(8,128)S(1)}, f32[48,32,128]{2,1,0:T(8,128)S(1)}, f32[6,24,8,128]{3,2,1,0:T(8,128)...) custom-call(f32[2,32,32,128]{3,2,1,0:T(8,128)S(1)} %get-tuple-element.49.own, ...), custom_call_target="tpu_custom_call" | custom-call | flops 200000000 | bytes 8000000 | tf_op jit(solution)/shard_map/viscosity/pallas_call | solution.py:395
  62.0 3.0 %down.2 = (f32[1,48,32,128]{3,2,1,0:T(8,128)S(1)}, f32[1,48,32,128]{3,2,1,0:T(8,128)S(1)}, f32[1,24,8,128]{3,2,1,0:T(8,128)S(1)}, f32[1,24,8,128]{3,2,1,0:T(8,128)S(1)}, f32[20,8,128]{2,1,0:T(8,128)S(1)}) custom-call(f32[2,32,32,128]{3,2,1,0:T(8,128)S(1)} %get-tuple-element.49.own, f32[2,7,32,128]{3,2,1,0:T(8,128)S(1)} %collective-permute-done.11.near, ...), custom_call_target="tpu_custom_call" | custom-call | flops 200000000 | bytes 8000000 | tf_op jit(solution)/shard_map/down/pallas_call | solution.py:481
  65.0 0.8 collective-permute-done.6.beyond
  65.9 4.7 %down.3 = (f32[2,48,32,128]{3,2,1,0:T(8,128)S(1)}, f32[2,48,32,128]{3,2,1,0:T(8,128)S(1)}, f32[2,24,8,128]{3,2,1,0:T(8,128)S(1)}, f32[2,24,8,128]{3,2,1,0:T(8,128)S(1)}, f32[20,8,128]{2,1,0:T(8,128)S(1)}) custom-call(f32[2,32,32,128]{3,2,1,0:T(8,128)S(1)} %get-tuple-element.43.own, f32[2,7,32,128]{3,2,1,0:T(8,128)S(1)} %collective-permute-done.5.near, ...), custom_call_target="tpu_custom_call" | custom-call | flops 200000000 | bytes 8000000 | tf_op jit(solution)/shard_map/down/pallas_call | solution.py:481
  70.7 1.3 %collective-permute-done.13.refs_1_ = f32[20,8,128]{2,1,0:T(8,128)S(1)} collective-permute-done((f32[20,8,128]{2,1,0:T(8,128)S(1)}, f32[20,8,128]{2,1,0:T(8,128)S(1)}, u32[]{:S(2)}, u32[]{:S(2)}) %collective-permute-start.13) | collective-permute-done | bytes 81952 | tf_op jit(solution)/shard_map/ppermute | solution.py:716
  72.0 4.0 %collective-permute-start.14 = (f32[22,8,128]{2,1,0:T(8,128)S(1)}, f32[22,8,128]{2,1,0:T(8,128)S(1)}, u32[]{:S(2)}, u32[]{:S(2)}) collective-permute-start(f32[22,8,128]{2,1,0:T(8,128)S(1)} %pad_maximum_fusion), channel_id=1, source_target_pairs={{1,2},{2,1},{3,4},{4,3},{5,6},{6,5},{7,8},{8,7},{9,10},{10,9},{11,... | collective-permute-start | bytes 270344 | tf_op jit(solution)/shard_map/ppermute | solution.py:720
  76.0 2.8 %collective-permute-start.15 = (f32[20,8,128]{2,1,0:T(8,128)S(1)}, f32[20,8,128]{2,1,0:T(8,128)S(1)}, u32[]{:S(2)}, u32[]{:S(2)}) collective-permute-start(f32[20,8,128]{2,1,0:T(8,128)S(1)} %get-tuple-element.60.refs_0_), channel_id=1, source_target_pairs={{1,4},{3,6},{4,1},{5,8},{6,3},{7,10},{8,5},{9,12},{10,7},{11,14},{... | collective-permute-start | bytes 245768 | tf_op jit(solution)/shard_map/ppermute | solution.py:736
  78.8 3.8 %collective-permute-done.15.refs_3_ = f32[20,8,128]{2,1,0:T(8,128)S(1)} collective-permute-done((f32[20,8,128]{2,1,0:T(8,128)S(1)}, f32[20,8,128]{2,1,0:T(8,128)S(1)}, u32[]{:S(2)}, u32[]{:S(2)}) %collective-permute-start.15) | collective-permute-done | bytes 81952 | tf_op jit(solution)/shard_map/ppermute | solution.py:736
  82.6 1.3 %collective-permute-done.16.refs_4_ = f32[22,8,128]{2,1,0:T(8,128)S(1)} collective-permute-done((f32[22,8,128]{2,1,0:T(8,128)S(1)}, f32[22,8,128]{2,1,0:T(8,128)S(1)}, u32[]{:S(2)}, u32[]{:S(2)}) %collective-permute-start.16) | collective-permute-done | bytes 90144 | tf_op jit(solution)/shard_map/ppermute | solution.py:716
  83.9 9.9 %up.1 = f32[4,3,32,1024]{3,2,1,0:T(8,128)} custom-call(f32[20,8,128]{2,1,0:T(8,128)S(1)} %get-tuple-element.60.refs_0_, f32[20,8,128]{2,1,0:T(8,128)S(1)} %collective-permute-done.13.refs_1_, f32[22,8,128]{2,1,0:T(8,128)S(1)} %collective-permute-done.14.refs_2_, f32[20,8,128]{2,1,0:T(8,128)S(1)} %collective-permute-done.15.refs_3_, ...), custom_call_target="tpu_custom_call" | custom-call | flops 400000000 | bytes 16000000 | tf_op jit(solution)/shard_map/up/pallas_call | solution.py:667
  (15 shorter events, 0.4 us)
Async XLA Ops:
  0.0 4.7 %collective-permute-start.1 = (f32[4,3,32,1024]{3,2,1,0:T(8,128)}, f32[4,3,32,1024]{3,2,1,0:T(8,128)S(1)}, u32[]{:S(2)}, u32[]{:S(2)}) collective-permute-start(f32[4,3,32,1024]{3,2,1,0:T(8,128)} %refs_1_.1), channel_id=1, source_target_pairs={{0,1},{1,0},{2,3},{3,2},{4,5},{5,4},{6,7},{7,6},{8,9},{9,8},{10,11... | collective-permute-start | bytes 4718600 | tf_op jit(solution)/shard_map/ppermute | solution.py:698
  0.7 4.0 %collective-permute-start = (f32[4,32,1024]{2,1,0:T(8,128)}, f32[4,32,1024]{2,1,0:T(8,128)S(1)}, u32[]{:S(2)}, u32[]{:S(2)}) collective-permute-start(f32[4,32,1024]{2,1,0:T(8,128)} %refs_0_.1), channel_id=1, source_target_pairs={{0,1},{1,0},{2,3},{3,2},{4,5},{5,4},{6,7},{7,6},{8,9},{9,8},{10,11... | collective-permute-start | bytes 1572872 | tf_op jit(solution)/shard_map/ppermute | solution.py:698
  3.0 8.4 %collective-permute-start.7 = (f32[1,2,32,1024]{3,2,1,0:T(8,128)S(1)}, f32[1,2,32,1024]{3,2,1,0:T(8,128)S(1)}, u32[]{:S(2)}, u32[]{:S(2)}) collective-permute-start(f32[1,2,32,1024]{3,2,1,0:T(8,128)S(1)} %pack.4), channel_id=1, source_target_pairs={{0,6},{1,7},{2,4},{3,5},{4,2},{5,3},{6,0},{7,1},{8,14},{9,15},{10,... | collective-permute-start | bytes 786440 | tf_op jit(solution)/shard_map/ppermute | solution.py:712
  5.5 11.5 %collective-permute-start.8 = (f32[1,2,32,1024]{3,2,1,0:T(8,128)S(1)}, f32[1,2,32,1024]{3,2,1,0:T(8,128)S(1)}, u32[]{:S(2)}, u32[]{:S(2)}) collective-permute-start(f32[1,2,32,1024]{3,2,1,0:T(8,128)S(1)} %get-tuple-element.46), channel_id=1, source_target_pairs={{0,6},{1,7},{2,4},{3,5},{4,2},{5,3},{6,0},{7,1},{8,14},{9,15},{10,... | collective-permute-start | bytes 786440 | tf_op jit(solution)/shard_map/ppermute | solution.py:712
  6.3 23.6 %collective-permute-start.9 = (f32[2,2,32,1024]{3,2,1,0:T(8,128)S(1)}, f32[2,2,32,1024]{3,2,1,0:T(8,128)S(1)}, u32[]{:S(2)}, u32[]{:S(2)}) collective-permute-start(f32[2,2,32,1024]{3,2,1,0:T(8,128)S(1)} %get-tuple-element.47), channel_id=1, source_target_pairs={{0,4},{1,5},{2,6},{3,7},{4,0},{5,1},{6,2},{7,3},{8,12},{9,13},{10,... | collective-permute-start | bytes 1572872 | tf_op jit(solution)/shard_map/ppermute | solution.py:712
  7.0 22.9 %collective-permute-start.10 = (f32[2,2,32,1024]{3,2,1,0:T(8,128)S(1)}, f32[2,2,32,1024]{3,2,1,0:T(8,128)S(1)}, u32[]{:S(2)}, u32[]{:S(2)}) collective-permute-start(f32[2,2,32,1024]{3,2,1,0:T(8,128)S(1)} %get-tuple-element.48), channel_id=1, source_target_pairs={{0,2},{1,3},{2,0},{3,1},{4,6},{5,7},{6,4},{7,5},{8,10},{9,11},{10,... | collective-permute-start | bytes 1572872 | tf_op jit(solution)/shard_map/ppermute | solution.py:712
  9.0 30.5 %collective-permute-start.2 = (f32[2,2,32,1024]{3,2,1,0:T(8,128)S(1)}, f32[2,2,32,1024]{3,2,1,0:T(8,128)S(1)}, u32[]{:S(2)}, u32[]{:S(2)}) collective-permute-start(f32[2,2,32,1024]{3,2,1,0:T(8,128)S(1)} %get-tuple-element.40), channel_id=1, source_target_pairs={{0,6},{1,7},{2,4},{3,5},{4,2},{5,3},{6,0},{7,1},{8,14},{9,15},{10,... | collective-permute-start | bytes 1572872 | tf_op jit(solution)/shard_map/ppermute | solution.py:712
  11.4 42.6 %collective-permute-start.3 = (f32[2,2,32,1024]{3,2,1,0:T(8,128)S(1)}, f32[2,2,32,1024]{3,2,1,0:T(8,128)S(1)}, u32[]{:S(2)}, u32[]{:S(2)}) collective-permute-start(f32[2,2,32,1024]{3,2,1,0:T(8,128)S(1)} %get-tuple-element.41), channel_id=1, source_target_pairs={{0,4},{1,5},{2,6},{3,7},{4,0},{5,1},{6,2},{7,3},{8,12},{9,13},{10,... | collective-permute-start | bytes 1572872 | tf_op jit(solution)/shard_map/ppermute | solution.py:712
  17.0 37.0 %collective-permute-start.4 = (f32[2,2,32,1024]{3,2,1,0:T(8,128)S(1)}, f32[2,2,32,1024]{3,2,1,0:T(8,128)S(1)}, u32[]{:S(2)}, u32[]{:S(2)}) collective-permute-start(f32[2,2,32,1024]{3,2,1,0:T(8,128)S(1)} %get-tuple-element.42), channel_id=1, source_target_pairs={{0,2},{1,3},{2,0},{3,1},{4,6},{5,7},{6,4},{7,5},{8,10},{9,11},{10,... | collective-permute-start | bytes 1572872 | tf_op jit(solution)/shard_map/ppermute | solution.py:712
  32.3 27.5 %collective-permute-start.11 = (f32[2,7,32,128]{3,2,1,0:T(8,128)S(1)}, f32[2,7,32,128]{3,2,1,0:T(8,128)S(1)}, u32[]{:S(2)}, u32[]{:S(2)}) collective-permute-start(f32[2,7,32,128]{3,2,1,0:T(8,128)S(1)} %get-tuple-element.50), channel_id=1, source_target_pairs={{0,1},{1,0},{2,3},{3,2},{4,5},{5,4},{6,7},{7,6},{8,9},{9,8},{10,11... | collective-permute-start | bytes 688136 | tf_op jit(solution)/shard_map/ppermute | solution.py:716
  33.4 26.4 %collective-permute-start.12 = (f32[2,7,32,128]{3,2,1,0:T(8,128)S(1)}, f32[2,7,32,128]{3,2,1,0:T(8,128)S(1)}, u32[]{:S(2)}, u32[]{:S(2)}) collective-permute-start(f32[2,7,32,128]{3,2,1,0:T(8,128)S(1)} %get-tuple-element.51), channel_id=1, source_target_pairs={{1,2},{2,1},{3,4},{4,3},{5,6},{6,5},{7,8},{8,7},{9,10},{10,9},{11,... | collective-permute-start | bytes 688136 | tf_op jit(solution)/shard_map/ppermute | solution.py:720
  56.1 8.9 %collective-permute-start.5 = (f32[2,7,32,128]{3,2,1,0:T(8,128)S(1)}, f32[2,7,32,128]{3,2,1,0:T(8,128)S(1)}, u32[]{:S(2)}, u32[]{:S(2)}) collective-permute-start(f32[2,7,32,128]{3,2,1,0:T(8,128)S(1)} %get-tuple-element.44), channel_id=1, source_target_pairs={{0,1},{1,0},{2,3},{3,2},{4,5},{5,4},{6,7},{7,6},{8,9},{9,8},{10,11... | collective-permute-start | bytes 688136 | tf_op jit(solution)/shard_map/ppermute | solution.py:716
  56.6 9.2 %collective-permute-start.6 = (f32[2,7,32,128]{3,2,1,0:T(8,128)S(1)}, f32[2,7,32,128]{3,2,1,0:T(8,128)S(1)}, u32[]{:S(2)}, u32[]{:S(2)}) collective-permute-start(f32[2,7,32,128]{3,2,1,0:T(8,128)S(1)} %get-tuple-element.45), channel_id=1, source_target_pairs={{1,2},{2,1},{3,4},{4,3},{5,6},{6,5},{7,8},{8,7},{9,10},{10,9},{11,... | collective-permute-start | bytes 688136 | tf_op jit(solution)/shard_map/ppermute | solution.py:720
  70.6 1.3 %collective-permute-start.13 = (f32[20,8,128]{2,1,0:T(8,128)S(1)}, f32[20,8,128]{2,1,0:T(8,128)S(1)}, u32[]{:S(2)}, u32[]{:S(2)}) collective-permute-start(f32[20,8,128]{2,1,0:T(8,128)S(1)} %get-tuple-element.60.refs_0_), channel_id=1, source_target_pairs={{0,1},{1,0},{2,3},{3,2},{4,5},{5,4},{6,7},{7,6},{8,9},{9,8},{10,11... | collective-permute-start | bytes 245768 | tf_op jit(solution)/shard_map/ppermute | solution.py:716
  72.0 10.7 %collective-permute-start.14 = (f32[22,8,128]{2,1,0:T(8,128)S(1)}, f32[22,8,128]{2,1,0:T(8,128)S(1)}, u32[]{:S(2)}, u32[]{:S(2)}) collective-permute-start(f32[22,8,128]{2,1,0:T(8,128)S(1)} %pad_maximum_fusion), channel_id=1, source_target_pairs={{1,2},{2,1},{3,4},{4,3},{5,6},{6,5},{7,8},{8,7},{9,10},{10,9},{11,... | collective-permute-start | bytes 270344 | tf_op jit(solution)/shard_map/ppermute | solution.py:720
  76.0 6.7 %collective-permute-start.15 = (f32[20,8,128]{2,1,0:T(8,128)S(1)}, f32[20,8,128]{2,1,0:T(8,128)S(1)}, u32[]{:S(2)}, u32[]{:S(2)}) collective-permute-start(f32[20,8,128]{2,1,0:T(8,128)S(1)} %get-tuple-element.60.refs_0_), channel_id=1, source_target_pairs={{1,4},{3,6},{4,1},{5,8},{6,3},{7,10},{8,5},{9,12},{10,7},{11,14},{... | collective-permute-start | bytes 245768 | tf_op jit(solution)/shard_map/ppermute | solution.py:736
  82.6 1.3 %collective-permute-start.16 = (f32[22,8,128]{2,1,0:T(8,128)S(1)}, f32[22,8,128]{2,1,0:T(8,128)S(1)}, u32[]{:S(2)}, u32[]{:S(2)}) collective-permute-start(f32[22,8,128]{2,1,0:T(8,128)S(1)} %collective-permute-done.14.refs_2_), channel_id=1, source_target_pairs={{0,1},{1,0},{2,3},{3,2},{4,5},{5,4},{6,7},{7,6},{8,9},{9,8},{10,11... | collective-permute-start | bytes 270344 | tf_op jit(solution)/shard_map/ppermute | solution.py:716

commit v2 on v1

--- a/solution.py
+++ b/solution.py
@@ -235,16 +235,6 @@
     return slot
 
 
-def pick(viscosity, velocity, block, fields):
-    parts, at = [], 0
-    if fields[0] is None:
-        parts.append((pl.ds(0, 1), viscosity.at[pl.ds(block, 1)]))
-        fields, at = fields[1:], 1
-    if fields:
-        parts.append((pl.ds(at, len(fields)), velocity.at[block, pl.ds(fields[0], len(fields))]))
-    return parts
-
-
 def load_kernel(*refs):
     count = (len(refs) - 1) // 2
     copies = [
@@ -266,6 +256,29 @@
     )(*arrays)
 
 
+def early_kernel(members, fields, turn, source, viscosity, velocity, out, sems):
+    group, member, _ = place_in_mesh()
+    blocks = viscosity.shape[0]
+    slot = slot_for(source, group * members * blocks, blocks, member ^ turn, member)
+    copies = []
+    for f, field in enumerate(fields):
+        own = viscosity.at[slot] if field is None else velocity.at[slot, field]
+        copies.append(pltpu.make_async_copy(own, out.at[0, f], sems.at[f]))
+    finish(start(copies))
+
+
+def early_pack(source, viscosity, velocity, fields, members, turn):
+    return pl.pallas_call(
+        functools.partial(early_kernel, members, fields, turn),
+        in_specs=[SCALARS, ANY, ANY],
+        out_specs=WHOLE,
+        out_shape=jax.ShapeDtypeStruct((1, len(fields), *viscosity.shape[-2:]), F32),
+        scratch_shapes=[pltpu.SemaphoreType.DMA((len(fields),))],
+        compiler_params=pltpu.CompilerParams(vmem_limit_bytes=8 * MEGA),
+        name="early",
+    )(source, viscosity, velocity)
+
+
 def pack_kernel(members, fields, sends, source, *refs):
     raw, outs = refs[: -len(sends)], refs[-len(sends) :]
     blocks = raw[0].shape[0]
@@ -291,32 +304,32 @@
 
 
 def assemble_kernel(members, fields, sends, source, viscosity, velocity, viscosity_other, velocity_other, *refs):
-    received, (own, facing, outer, tall, turned, sems) = refs[: len(sends)], refs[len(sends) :]
+    received, (own, facing, outer, tall, turned) = refs[: len(sends)], refs[len(sends) :]
     blocks = viscosity.shape[0]
     edge = own.shape[1]
     group, member, _ = place_in_mesh()
     base = group * members * blocks
 
-    def each_copy(act):
-        for j in range(blocks):
-            owner = lax.div(source[base + member * blocks + j] - base, blocks)
-            rows = pl.ds((j % 2) * 64 + (j // 2) * edge, edge)
-            for n, arrays in enumerate(((viscosity, velocity), (viscosity_other, velocity_other))):
-
-                @pl.when(owner == member ^ n)
-                def _(arrays=arrays):
-                    for f, (goal, part) in enumerate(pick(*arrays, j, fields)):
-                        act(pltpu.make_async_copy(part, tall.at[goal, rows], sems.at[j, f]))
-
-            for part, (turn, owners) in zip(received, sends):
-                for at, n in enumerate(owners):
-
-                    @pl.when(owner == member ^ turn ^ n)
-                    def _(part=part, at=at):
-                        act(pltpu.make_async_copy(part.at[at], tall.at[:, rows], sems.at[j, 0]))
-
-    each_copy(lambda copy: copy.start())
-    each_copy(lambda copy: copy.wait())
+    def gather(rows, values):
+        for f, field in enumerate(fields):
+            tall[f, rows] = values(f, field)
+
+    for j in range(blocks):
+        owner = lax.div(source[base + member * blocks + j] - base, blocks)
+        rows = pl.ds((j % 2) * 64 + (j // 2) * edge, edge)
+        for n, (visc, vel) in enumerate(((viscosity, velocity), (viscosity_other, velocity_other))):
+
+            @pl.when(owner == member ^ n)
+            def _(visc=visc, vel=vel):
+                gather(rows, lambda f, field: visc[j] if field is None else vel[j, field])
+
+        for part, (turn, owners) in zip(received, sends):
+            for at, n in enumerate(owners):
+
+                @pl.when(owner == member ^ turn ^ n)
+                def _(part=part, at=at):
+                    gather(rows, lambda f, field: part[at, f])
+
     for f in range(len(fields)):
         for at in range(edge * edge // LANES):
             turned[f, pl.ds(at * LANES, LANES)] = tall[f, :, pl.ds(at * LANES, LANES)].T
@@ -341,7 +354,6 @@
         scratch_shapes=[
             pltpu.VMEM((width, LANES, flat), F32),
             vmem(width, flat),
-            pltpu.SemaphoreType.DMA((raw[0].shape[0], 2)),
         ],
         out_shape=[shaped(width, layers, rows) for layers in (edge, HALO, HALO)],
         compiler_params=pltpu.CompilerParams(vmem_limit_bytes=16 * MEGA),
@@ -363,7 +375,7 @@
     copy_layers(target, jnp.where(odd, high, low), beyond, at, HALO)
 
 
-def viscosity_kernel(total_x, own, near, beyond, coef, scale, back, coef1, scale1, back1, nu2, nu, nu1, sums):
+def viscosity_kernel(total_x, own, beyond, near, coef, scale, back, coef1, scale1, back1, nu2, nu, nu1, sums):
     width = own.shape[1]
     layers, layers1 = width + 2 * BASE0, width // 2 + 2 * BASE1
     _, _, me = place_in_mesh()
@@ -411,7 +423,7 @@
 
 
 def down_kernel(
-    comp_at, first_field, own, near, beyond, coef, scale, back, coef1, scale1, back1, *refs,
+    comp_at, first_field, own, beyond, near, coef, scale, back, coef1, scale1, back1, *refs,
 ):
     before, (A, right, B1, right1, message, B, sums, rhs1, A1) = refs[0], refs[1:]
     comps = len(comp_at)
@@ -499,7 +511,7 @@
 
 
 def up_kernel(total_x, parts, *refs):
-    (message, beside, beyond, far, other), refs = refs[:5], refs[5:]
+    (far, beyond, message, beside, other), refs = refs[:5], refs[5:]
     coef, coef1, refs = refs[0], refs[1], refs[2:]
     comps = []
     for part in parts:
@@ -694,8 +706,8 @@
     total_x = count * edge
     turns = turn_order(members)
     pairs = [(m, m ^ 1) for m in range(members)]
-    own_raw = load(viscosity_old, velocity_old)
-    raw = (*own_raw, *(lax.ppermute(array, "dev", pairs) for array in (viscosity_old, velocity_old)))
+    in_hbm = [pltpu.with_memory_space_constraint(array, pltpu.HBM) for array in (viscosity_old, velocity_old)]
+    raw = (*load(viscosity_old, velocity_old), *(lax.ppermute(array, "dev", pairs) for array in (viscosity_old, velocity_old)))
     source = pltpu.with_memory_space_constraint(source, pltpu.HBM)
 
     chunks = ((None, 0), (1, 2))
@@ -706,7 +718,7 @@
     for fields, plan in zip(chunks, plans):
         packed = []
         if plan[0] in early:
-            packed += pack(source, own_raw, fields, members, early)
+            packed.append(early_pack(source, *in_hbm, fields, members, turns[0]))
         packed += pack(source, raw, fields, members, plan[len(packed) :])
         received.append(
             [lax.ppermute(sent, "dev", [(m, m ^ turn) for m in range(members)]) for (turn, _), sent in zip(plan, packed)]
@@ -723,7 +735,7 @@
     for fields, plan, slots in zip(chunks, plans, received):
         grid, facing, outer = assemble(source, raw, fields, slots, members, plan)
         beyond = swap_outward(outer, 1)
-        grids.append((grid, swap(facing, 1), beyond))
+        grids.append((grid, beyond, swap(facing, 1)))
     *weights, sent = viscosity_weights(grids[0], total_x)
     kept = []
     for fields, arrays in zip(chunks, grids):
@@ -739,7 +751,7 @@
     came, far = lax.optimization_barrier((beyond, far))
     other = swap(came, 1)
     widths = tuple(state[0].shape[0] for state in kept)
-    return up((sent, beside, beyond, far, other), (weights[0], weights[3]), kept, widths, edge, total_x)
+    return up((far, beyond, sent, beside, other), (weights[0], weights[3]), kept, widths, edge, total_x)
 
 
 def turn_order(members):

time: 94.9 us -> 94.1 us (level)
  waiting for transfers between devices: 45.9 us -> 43 us
  starting transfers between devices: 19.5 us -> 20.9 us
    pallas_call x0 -> x1, Pallas kernels: none -> 1.67 us  [early_pack(): pl.pallas_call(functools.partial(early_kernel, members, fields, turn), in...]
    ppermute x3, starting transfers between devices: 10.1 us -> 11.4 us  [swap_outward(): lax.ppermute(array, axes, [(i, to) for i, to in goals if 0 <= to < count])]
    ppermute x4, starting transfers between devices: 1.76 us -> 0.67 us  [swap(): return lax.ppermute(array, axes, [(i, i ^ hop) for i in range(count)])]
    ppermute x7, starting transfers between devices: 4.09 us -> 5.07 us  [local(): lax.ppermute(sent, 'dev', [(m, m ^ turn) for m in range(members)])]
    ppermute x2, waiting for transfers between devices: 1.6 us -> 0.63 us  [local(): lax.ppermute(array, 'dev', pairs)]
    pallas_call x3 -> x2, Pallas kernels: 2.27 us -> 1.56 us  [pack(): pl.pallas_call(functools.partial(pack_kernel, members, fields, sends), in...]
  transfers between devices with their start and end apart: 17 -> 17, of which waited for: 10 -> 9; matrix products, arithmetic and copies ran while one was open for 0% -> 0% of each run, Pallas kernels for 14% -> 15%
where the time goes in v2:
time: 94.1 us; the launch traced here: 92.8 us
  waiting for transfers between devices  43 us (46%)
  Pallas kernels  28.5 us (30%)
  starting transfers between devices  20.9 us (22%)
    ppermute x7, waiting for transfers between devices, local(): lax.ppermute(sent, 'dev', [(m, m ^ turn) for m in range(members)])  36.3 us
    ppermute x3, starting transfers between devices, swap_outward(): lax.ppermute(array, axes, [(i, to) for i, to in goals if 0 <= to < count])  11.4 us
    pallas_call x1, Pallas kernels, up(): pl.pallas_call(functools.partial(up_kernel, total_x, parts), in_specs=[WH...  9.89 us
    pallas_call x2, Pallas kernels, down(): pl.pallas_call(functools.partial(down_kernel, comp_at, first_field), in_s...  7.76 us
    ppermute x7, starting transfers between devices, local(): lax.ppermute(sent, 'dev', [(m, m ^ turn) for m in range(members)])  5.07 us
    pallas_call x2, Pallas kernels, assemble(): pl.pallas_call(functools.partial(assemble_kernel, members, fields, sends)...  3.85 us
    ppermute x1, waiting for transfers between devices, local(): lax.ppermute(sent, axes, [(i, to) for i, to in hops if 0 <= to < count])  3.57 us
    ppermute x1, starting transfers between devices, local(): lax.ppermute(sent, axes, [(i, to) for i, to in hops if 0 <= to < count])  3.08 us
  transfers between devices with their start and end apart: 17, of which 9 were waited for; matrix products, arithmetic and copies ran while one was open for 0% of the time, Pallas kernels for 15%

profile of v2, /device:TPU:7, one launch (start us, length us, event | category | flops | bytes accessed | tf_op | source)
XLA Modules:
  0.0 92.8 jit_solution(15869092807157983157)
XLA Ops:
  0.0 0.7 collective-permute-start.1
  0.7 1.7 %early.1 = f32[1,2,32,1024]{3,2,1,0:T(8,128)S(1)} custom-call(s32[128]{0:T(128)} %source.9, f32[4,32,1024]{2,1,0:T(8,128)} %viscosity.2, f32[4,3,32,1024]{3,2,1,0:T(8,128)} %velocity.1), custom_call_target="tpu_custom_call" | custom-call | tf_op jit(solution)/shard_map/early/pallas_call | solution.py:271
  2.4 1.6 %load.1 = (f32[4,32,1024]{2,1,0:T(8,128)S(1)}, f32[4,3,32,1024]{3,2,1,0:T(8,128)S(1)}) custom-call(f32[4,32,1024]{2,1,0:T(8,128)} %viscosity.2, f32[4,3,32,1024]{3,2,1,0:T(8,128)} %velocity.1), custom_call_target="tpu_custom_call" | custom-call | tf_op jit(solution)/shard_map/load/pallas_call | solution.py:248
  4.0 0.6 collective-permute-done.refs_2_.viscosity_other
  4.7 0.8 pack.3
  5.5 1.8 %collective-permute-start.8 = (f32[1,2,32,1024]{3,2,1,0:T(8,128)S(1)}, f32[1,2,32,1024]{3,2,1,0:T(8,128)S(1)}, u32[]{:S(2)}, u32[]{:S(2)}) collective-permute-start(f32[1,2,32,1024]{3,2,1,0:T(8,128)S(1)} %get-tuple-element.46), channel_id=1, source_target_pairs={{0,6},{1,7},{2,4},{3,5},{4,2},{5,3},{6,0},{7,1},{8,14},{9,15},{10,... | collective-permute-start | bytes 786440 | tf_op jit(solution)/shard_map/ppermute | solution.py:724
  7.3 0.2 collective-permute-start.9
  7.5 0.7 collective-permute-start.10
  8.2 0.8 pack.2
  9.0 1.8 %collective-permute-start.2 = (f32[2,2,32,1024]{3,2,1,0:T(8,128)S(1)}, f32[2,2,32,1024]{3,2,1,0:T(8,128)S(1)}, u32[]{:S(2)}, u32[]{:S(2)}) collective-permute-start(f32[2,2,32,1024]{3,2,1,0:T(8,128)S(1)} %get-tuple-element.40), channel_id=1, source_target_pairs={{0,6},{1,7},{2,4},{3,5},{4,2},{5,3},{6,0},{7,1},{8,14},{9,15},{10,... | collective-permute-start | bytes 1572872 | tf_op jit(solution)/shard_map/ppermute | solution.py:724
  10.8 0.2 collective-permute-start.3
  11.0 5.3 %collective-permute-done.8.refs_1_ = f32[1,2,32,1024]{3,2,1,0:T(8,128)S(1)} collective-permute-done((f32[1,2,32,1024]{3,2,1,0:T(8,128)S(1)}, f32[1,2,32,1024]{3,2,1,0:T(8,128)S(1)}, u32[]{:S(2)}, u32[]{:S(2)}) %collective-permute-start.8) | collective-permute-done | bytes 262176 | tf_op jit(solution)/shard_map/ppermute | solution.py:724
  16.3 0.3 collective-permute-start.4
  16.6 12.6 %collective-permute-done.9.refs_2_ = f32[2,2,32,1024]{3,2,1,0:T(8,128)S(1)} collective-permute-done((f32[2,2,32,1024]{3,2,1,0:T(8,128)S(1)}, f32[2,2,32,1024]{3,2,1,0:T(8,128)S(1)}, u32[]{:S(2)}, u32[]{:S(2)}) %collective-permute-start.9) | collective-permute-done | bytes 524320 | tf_op jit(solution)/shard_map/ppermute | solution.py:724
  29.2 1.9 %assemble.3 = (f32[2,32,32,128]{3,2,1,0:T(8,128)S(1)}, f32[2,7,32,128]{3,2,1,0:T(8,128)S(1)}, f32[2,7,32,128]{3,2,1,0:T(8,128)S(1)}) custom-call(s32[128]{0:T(128)} %source.9, f32[4,32,1024]{2,1,0:T(8,128)S(1)} %get-tuple-element.38.refs_0_.viscosity, f32[4,3,32,1024]{3,2,1,0:T(8,128)S(1)} %get-tuple-element.39.refs_1_.velocity, ...), custom_call_target="tpu_custom_call" | custom-call | tf_op jit(solution)/shard_map/assemble/pallas_call | solution.py:350
  31.2 3.7 %collective-permute-start.11 = (f32[2,7,32,128]{3,2,1,0:T(8,128)S(1)}, f32[2,7,32,128]{3,2,1,0:T(8,128)S(1)}, u32[]{:S(2)}, u32[]{:S(2)}) collective-permute-start(f32[2,7,32,128]{3,2,1,0:T(8,128)S(1)} %get-tuple-element.50), channel_id=1, source_target_pairs={{1,2},{2,1},{3,4},{4,3},{5,6},{6,5},{7,8},{8,7},{9,10},{10,9},{11,... | collective-permute-start | bytes 688136 | tf_op jit(solution)/shard_map/ppermute | solution.py:732
  34.9 0.1 collective-permute-start.12
  35.0 6.3 %collective-permute-done.2.refs_0_ = f32[2,2,32,1024]{3,2,1,0:T(8,128)S(1)} collective-permute-done((f32[2,2,32,1024]{3,2,1,0:T(8,128)S(1)}, f32[2,2,32,1024]{3,2,1,0:T(8,128)S(1)}, u32[]{:S(2)}, u32[]{:S(2)}) %collective-permute-start.2) | collective-permute-done | bytes 524320 | tf_op jit(solution)/shard_map/ppermute | solution.py:724
  41.3 12.0 %collective-permute-done.3.refs_1_ = f32[2,2,32,1024]{3,2,1,0:T(8,128)S(1)} collective-permute-done((f32[2,2,32,1024]{3,2,1,0:T(8,128)S(1)}, f32[2,2,32,1024]{3,2,1,0:T(8,128)S(1)}, u32[]{:S(2)}, u32[]{:S(2)}) %collective-permute-start.3) | collective-permute-done | bytes 524320 | tf_op jit(solution)/shard_map/ppermute | solution.py:724
  53.3 1.9 %assemble.2 = (f32[2,32,32,128]{3,2,1,0:T(8,128)S(1)}, f32[2,7,32,128]{3,2,1,0:T(8,128)S(1)}, f32[2,7,32,128]{3,2,1,0:T(8,128)S(1)}) custom-call(s32[128]{0:T(128)} %source.9, f32[4,32,1024]{2,1,0:T(8,128)S(1)} %get-tuple-element.38.refs_0_.viscosity, f32[4,3,32,1024]{3,2,1,0:T(8,128)S(1)} %get-tuple-element.39.refs_1_.velocity, ...), custom_call_target="tpu_custom_call" | custom-call | tf_op jit(solution)/shard_map/assemble/pallas_call | solution.py:350
  55.3 3.6 %collective-permute-start.5 = (f32[2,7,32,128]{3,2,1,0:T(8,128)S(1)}, f32[2,7,32,128]{3,2,1,0:T(8,128)S(1)}, u32[]{:S(2)}, u32[]{:S(2)}) collective-permute-start(f32[2,7,32,128]{3,2,1,0:T(8,128)S(1)} %get-tuple-element.44), channel_id=1, source_target_pairs={{1,2},{2,1},{3,4},{4,3},{5,6},{6,5},{7,8},{8,7},{9,10},{10,9},{11,... | collective-permute-start | bytes 688136 | tf_op jit(solution)/shard_map/ppermute | solution.py:732
  59.0 2.2 %viscosity.3 = (f32[6,48,32,128]{3,2,1,0:T(8,128)S(1)}, f32[48,32,128]{2,1,0:T(8,128)S(1)}, f32[48,32,128]{2,1,0:T(8,128)S(1)}, f32[6,24,8,128]{3,2,1,0:T(8,128)...) custom-call(f32[2,32,32,128]{3,2,1,0:T(8,128)S(1)} %get-tuple-element.49.own, ...), custom_call_target="tpu_custom_call" | custom-call | flops 200000000 | bytes 8000000 | tf_op jit(solution)/shard_map/viscosity/pallas_call | solution.py:407
  61.2 3.0 %down.2 = (f32[1,48,32,128]{3,2,1,0:T(8,128)S(1)}, f32[1,48,32,128]{3,2,1,0:T(8,128)S(1)}, f32[1,24,8,128]{3,2,1,0:T(8,128)S(1)}, f32[1,24,8,128]{3,2,1,0:T(8,128)S(1)}, f32[20,8,128]{2,1,0:T(8,128)S(1)}) custom-call(f32[2,32,32,128]{3,2,1,0:T(8,128)S(1)} %get-tuple-element.49.own, f32[2,7,32,128]{3,2,1,0:T(8,128)S(1)} %collective-permute-done.11.beyond, ...), custom_call_target="tpu_custom_call" | custom-call | flops 200000000 | bytes 8000000 | tf_op jit(solution)/shard_map/down/pallas_call | solution.py:493
  64.2 0.3 collective-permute-done.5.beyond
  64.5 4.7 %down.3 = (f32[2,48,32,128]{3,2,1,0:T(8,128)S(1)}, f32[2,48,32,128]{3,2,1,0:T(8,128)S(1)}, f32[2,24,8,128]{3,2,1,0:T(8,128)S(1)}, f32[2,24,8,128]{3,2,1,0:T(8,128)S(1)}, f32[20,8,128]{2,1,0:T(8,128)S(1)}) custom-call(f32[2,32,32,128]{3,2,1,0:T(8,128)S(1)} %get-tuple-element.43.own, f32[2,7,32,128]{3,2,1,0:T(8,128)S(1)} %collective-permute-done.5.beyond, ...), custom_call_target="tpu_custom_call" | custom-call | flops 200000000 | bytes 8000000 | tf_op jit(solution)/shard_map/down/pallas_call | solution.py:493
  69.3 0.5 collective-permute-start.13
  69.8 0.9 collective-permute-done.13.refs_3_
  70.7 4.1 %collective-permute-start.14 = (f32[22,8,128]{2,1,0:T(8,128)S(1)}, f32[22,8,128]{2,1,0:T(8,128)S(1)}, u32[]{:S(2)}, u32[]{:S(2)}) collective-permute-start(f32[22,8,128]{2,1,0:T(8,128)S(1)} %pad_maximum_fusion), channel_id=1, source_target_pairs={{1,2},{2,1},{3,4},{4,3},{5,6},{6,5},{7,8},{8,7},{9,10},{10,9},{11,... | collective-permute-start | bytes 270344 | tf_op jit(solution)/shard_map/ppermute | solution.py:732
  74.8 3.1 %collective-permute-start.15 = (f32[20,8,128]{2,1,0:T(8,128)S(1)}, f32[20,8,128]{2,1,0:T(8,128)S(1)}, u32[]{:S(2)}, u32[]{:S(2)}) collective-permute-start(f32[20,8,128]{2,1,0:T(8,128)S(1)} %get-tuple-element.60.refs_2_), channel_id=1, source_target_pairs={{1,4},{3,6},{4,1},{5,8},{6,3},{7,10},{8,5},{9,12},{10,7},{11,14},{... | collective-permute-start | bytes 245768 | tf_op jit(solution)/shard_map/ppermute | solution.py:748
  77.9 3.6 %collective-permute-done.15.refs_0_ = f32[20,8,128]{2,1,0:T(8,128)S(1)} collective-permute-done((f32[20,8,128]{2,1,0:T(8,128)S(1)}, f32[20,8,128]{2,1,0:T(8,128)S(1)}, u32[]{:S(2)}, u32[]{:S(2)}) %collective-permute-start.15) | collective-permute-done | bytes 81952 | tf_op jit(solution)/shard_map/ppermute | solution.py:748
  81.5 1.3 %collective-permute-done.16.refs_4_ = f32[22,8,128]{2,1,0:T(8,128)S(1)} collective-permute-done((f32[22,8,128]{2,1,0:T(8,128)S(1)}, f32[22,8,128]{2,1,0:T(8,128)S(1)}, u32[]{:S(2)}, u32[]{:S(2)}) %collective-permute-start.16) | collective-permute-done | bytes 90144 | tf_op jit(solution)/shard_map/ppermute | solution.py:728
  82.8 9.9 %up.1 = f32[4,3,32,1024]{3,2,1,0:T(8,128)} custom-call(f32[20,8,128]{2,1,0:T(8,128)S(1)} %collective-permute-done.15.refs_0_, f32[22,8,128]{2,1,0:T(8,128)S(1)} %collective-permute-done.14.refs_1_, f32[20,8,128]{2,1,0:T(8,128)S(1)} %get-tuple-element.60.refs_2_, f32[20,8,128]{2,1,0:T(8,128)S(1)} %collective-permute-done.13.refs_3_, ...), custom_call_target="tpu_custom_call" | custom-call | flops 400000000 | bytes 16000000 | tf_op jit(solution)/shard_map/up/pallas_call | solution.py:679
  (15 shorter events, 0.2 us)
Async XLA Ops:
  0.0 4.7 %collective-permute-start.1 = (f32[4,3,32,1024]{3,2,1,0:T(8,128)}, f32[4,3,32,1024]{3,2,1,0:T(8,128)S(1)}, u32[]{:S(2)}, u32[]{:S(2)}) collective-permute-start(f32[4,3,32,1024]{3,2,1,0:T(8,128)} %velocity.1), channel_id=1, source_target_pairs={{0,1},{1,0},{2,3},{3,2},{4,5},{5,4},{6,7},{7,6},{8,9},{9,8},{10,11... | collective-permute-start | bytes 4718600 | tf_op jit(solution)/shard_map/ppermute | solution.py:710
  0.7 4.0 %collective-permute-start = (f32[4,32,1024]{2,1,0:T(8,128)}, f32[4,32,1024]{2,1,0:T(8,128)S(1)}, u32[]{:S(2)}, u32[]{:S(2)}) collective-permute-start(f32[4,32,1024]{2,1,0:T(8,128)} %viscosity.2), channel_id=1, source_target_pairs={{0,1},{1,0},{2,3},{3,2},{4,5},{5,4},{6,7},{7,6},{8,9},{9,8},{10,11... | collective-permute-start | bytes 1572872 | tf_op jit(solution)/shard_map/ppermute | solution.py:710
  2.4 8.4 %collective-permute-start.7 = (f32[1,2,32,1024]{3,2,1,0:T(8,128)S(1)}, f32[1,2,32,1024]{3,2,1,0:T(8,128)S(1)}, u32[]{:S(2)}, u32[]{:S(2)}) collective-permute-start(f32[1,2,32,1024]{3,2,1,0:T(8,128)S(1)} %early.1), channel_id=1, source_target_pairs={{0,6},{1,7},{2,4},{3,5},{4,2},{5,3},{6,0},{7,1},{8,14},{9,15},{10,... | collective-permute-start | bytes 786440 | tf_op jit(solution)/shard_map/ppermute | solution.py:724
  5.5 10.9 %collective-permute-start.8 = (f32[1,2,32,1024]{3,2,1,0:T(8,128)S(1)}, f32[1,2,32,1024]{3,2,1,0:T(8,128)S(1)}, u32[]{:S(2)}, u32[]{:S(2)}) collective-permute-start(f32[1,2,32,1024]{3,2,1,0:T(8,128)S(1)} %get-tuple-element.46), channel_id=1, source_target_pairs={{0,6},{1,7},{2,4},{3,5},{4,2},{5,3},{6,0},{7,1},{8,14},{9,15},{10,... | collective-permute-start | bytes 786440 | tf_op jit(solution)/shard_map/ppermute | solution.py:724
  7.3 22.0 %collective-permute-start.9 = (f32[2,2,32,1024]{3,2,1,0:T(8,128)S(1)}, f32[2,2,32,1024]{3,2,1,0:T(8,128)S(1)}, u32[]{:S(2)}, u32[]{:S(2)}) collective-permute-start(f32[2,2,32,1024]{3,2,1,0:T(8,128)S(1)} %get-tuple-element.47), channel_id=1, source_target_pairs={{0,4},{1,5},{2,6},{3,7},{4,0},{5,1},{6,2},{7,3},{8,12},{9,13},{10,... | collective-permute-start | bytes 1572872 | tf_op jit(solution)/shard_map/ppermute | solution.py:724
  7.5 21.7 %collective-permute-start.10 = (f32[2,2,32,1024]{3,2,1,0:T(8,128)S(1)}, f32[2,2,32,1024]{3,2,1,0:T(8,128)S(1)}, u32[]{:S(2)}, u32[]{:S(2)}) collective-permute-start(f32[2,2,32,1024]{3,2,1,0:T(8,128)S(1)} %get-tuple-element.48), channel_id=1, source_target_pairs={{0,2},{1,3},{2,0},{3,1},{4,6},{5,7},{6,4},{7,5},{8,10},{9,11},{10,... | collective-permute-start | bytes 1572872 | tf_op jit(solution)/shard_map/ppermute | solution.py:724
  9.0 32.3 %collective-permute-start.2 = (f32[2,2,32,1024]{3,2,1,0:T(8,128)S(1)}, f32[2,2,32,1024]{3,2,1,0:T(8,128)S(1)}, u32[]{:S(2)}, u32[]{:S(2)}) collective-permute-start(f32[2,2,32,1024]{3,2,1,0:T(8,128)S(1)} %get-tuple-element.40), channel_id=1, source_target_pairs={{0,6},{1,7},{2,4},{3,5},{4,2},{5,3},{6,0},{7,1},{8,14},{9,15},{10,... | collective-permute-start | bytes 1572872 | tf_op jit(solution)/shard_map/ppermute | solution.py:724
  10.8 42.6 %collective-permute-start.3 = (f32[2,2,32,1024]{3,2,1,0:T(8,128)S(1)}, f32[2,2,32,1024]{3,2,1,0:T(8,128)S(1)}, u32[]{:S(2)}, u32[]{:S(2)}) collective-permute-start(f32[2,2,32,1024]{3,2,1,0:T(8,128)S(1)} %get-tuple-element.41), channel_id=1, source_target_pairs={{0,4},{1,5},{2,6},{3,7},{4,0},{5,1},{6,2},{7,3},{8,12},{9,13},{10,... | collective-permute-start | bytes 1572872 | tf_op jit(solution)/shard_map/ppermute | solution.py:724
  16.3 37.0 %collective-permute-start.4 = (f32[2,2,32,1024]{3,2,1,0:T(8,128)S(1)}, f32[2,2,32,1024]{3,2,1,0:T(8,128)S(1)}, u32[]{:S(2)}, u32[]{:S(2)}) collective-permute-start(f32[2,2,32,1024]{3,2,1,0:T(8,128)S(1)} %get-tuple-element.42), channel_id=1, source_target_pairs={{0,2},{1,3},{2,0},{3,1},{4,6},{5,7},{6,4},{7,5},{8,10},{9,11},{10,... | collective-permute-start | bytes 1572872 | tf_op jit(solution)/shard_map/ppermute | solution.py:724
  31.2 27.8 %collective-permute-start.11 = (f32[2,7,32,128]{3,2,1,0:T(8,128)S(1)}, f32[2,7,32,128]{3,2,1,0:T(8,128)S(1)}, u32[]{:S(2)}, u32[]{:S(2)}) collective-permute-start(f32[2,7,32,128]{3,2,1,0:T(8,128)S(1)} %get-tuple-element.50), channel_id=1, source_target_pairs={{1,2},{2,1},{3,4},{4,3},{5,6},{6,5},{7,8},{8,7},{9,10},{10,9},{11,... | collective-permute-start | bytes 688136 | tf_op jit(solution)/shard_map/ppermute | solution.py:732
  34.9 24.1 %collective-permute-start.12 = (f32[2,7,32,128]{3,2,1,0:T(8,128)S(1)}, f32[2,7,32,128]{3,2,1,0:T(8,128)S(1)}, u32[]{:S(2)}, u32[]{:S(2)}) collective-permute-start(f32[2,7,32,128]{3,2,1,0:T(8,128)S(1)} %get-tuple-element.51), channel_id=1, source_target_pairs={{0,1},{1,0},{2,3},{3,2},{4,5},{5,4},{6,7},{7,6},{8,9},{9,8},{10,11... | collective-permute-start | bytes 688136 | tf_op jit(solution)/shard_map/ppermute | solution.py:728
  55.3 9.2 %collective-permute-start.5 = (f32[2,7,32,128]{3,2,1,0:T(8,128)S(1)}, f32[2,7,32,128]{3,2,1,0:T(8,128)S(1)}, u32[]{:S(2)}, u32[]{:S(2)}) collective-permute-start(f32[2,7,32,128]{3,2,1,0:T(8,128)S(1)} %get-tuple-element.44), channel_id=1, source_target_pairs={{1,2},{2,1},{3,4},{4,3},{5,6},{6,5},{7,8},{8,7},{9,10},{10,9},{11,... | collective-permute-start | bytes 688136 | tf_op jit(solution)/shard_map/ppermute | solution.py:732
  58.9 5.6 %collective-permute-start.6 = (f32[2,7,32,128]{3,2,1,0:T(8,128)S(1)}, f32[2,7,32,128]{3,2,1,0:T(8,128)S(1)}, u32[]{:S(2)}, u32[]{:S(2)}) collective-permute-start(f32[2,7,32,128]{3,2,1,0:T(8,128)S(1)} %get-tuple-element.45), channel_id=1, source_target_pairs={{0,1},{1,0},{2,3},{3,2},{4,5},{5,4},{6,7},{7,6},{8,9},{9,8},{10,11... | collective-permute-start | bytes 688136 | tf_op jit(solution)/shard_map/ppermute | solution.py:728
  69.3 1.4 %collective-permute-start.13 = (f32[20,8,128]{2,1,0:T(8,128)S(1)}, f32[20,8,128]{2,1,0:T(8,128)S(1)}, u32[]{:S(2)}, u32[]{:S(2)}) collective-permute-start(f32[20,8,128]{2,1,0:T(8,128)S(1)} %get-tuple-element.60.refs_2_), channel_id=1, source_target_pairs={{0,1},{1,0},{2,3},{3,2},{4,5},{5,4},{6,7},{7,6},{8,9},{9,8},{10,11... | collective-permute-start | bytes 245768 | tf_op jit(solution)/shard_map/ppermute | solution.py:728
  70.7 10.8 %collective-permute-start.14 = (f32[22,8,128]{2,1,0:T(8,128)S(1)}, f32[22,8,128]{2,1,0:T(8,128)S(1)}, u32[]{:S(2)}, u32[]{:S(2)}) collective-permute-start(f32[22,8,128]{2,1,0:T(8,128)S(1)} %pad_maximum_fusion), channel_id=1, source_target_pairs={{1,2},{2,1},{3,4},{4,3},{5,6},{6,5},{7,8},{8,7},{9,10},{10,9},{11,... | collective-permute-start | bytes 270344 | tf_op jit(solution)/shard_map/ppermute | solution.py:732
  74.8 6.7 %collective-permute-start.15 = (f32[20,8,128]{2,1,0:T(8,128)S(1)}, f32[20,8,128]{2,1,0:T(8,128)S(1)}, u32[]{:S(2)}, u32[]{:S(2)}) collective-permute-start(f32[20,8,128]{2,1,0:T(8,128)S(1)} %get-tuple-element.60.refs_2_), channel_id=1, source_target_pairs={{1,4},{3,6},{4,1},{5,8},{6,3},{7,10},{8,5},{9,12},{10,7},{11,14},{... | collective-permute-start | bytes 245768 | tf_op jit(solution)/shard_map/ppermute | solution.py:748
  81.5 1.3 %collective-permute-start.16 = (f32[22,8,128]{2,1,0:T(8,128)S(1)}, f32[22,8,128]{2,1,0:T(8,128)S(1)}, u32[]{:S(2)}, u32[]{:S(2)}) collective-permute-start(f32[22,8,128]{2,1,0:T(8,128)S(1)} %collective-permute-done.14.refs_1_), channel_id=1, source_target_pairs={{0,1},{1,0},{2,3},{3,2},{4,5},{5,4},{6,7},{7,6},{8,9},{9,8},{10,11... | collective-permute-start | bytes 270344 | tf_op jit(solution)/shard_map/ppermute | solution.py:728

commit v3 on v2

--- a/solution.py
+++ b/solution.py
@@ -25,6 +25,7 @@
 SIDE1 = 3
 FETCHED = SIDE1 - 1
 EDGES = 3 * FETCHED
+SPARE = 4
 REACH = 3
 MEGA = 1024 * 1024
 
@@ -381,7 +382,7 @@
     _, _, me = place_in_mesh()
     copy_layers(nu, BASE0, own, 0, width)
     copy_halos(nu, near, beyond, 0, width, me)
-    make_weights(0, beside0, nu, coef, scale, back, 2, layers - 2, me * width - BASE0, total_x, step=8)
+    make_weights(0, beside0, nu, coef, scale, back, 2, layers - 2, me * width - BASE0, total_x, step=11)
 
     def nu_sums(t):
         a, b = pair_y(nu[2 + 2 * t] + nu[3 + 2 * t])
@@ -433,8 +434,8 @@
     for c, at in enumerate(comp_at):
         copy_layers(A.at[c], BASE0, own, at, width)
         copy_halos(A.at[c], near, beyond, at, width, me)
-    sweep(beside0, A, B, coef, right, comps, 2, layers - 2, scale=scale, step=11)
-    sweep(beside0, B, A, coef, right, comps, 3, layers - 3, step=14)
+    sweep(beside0, A, B, coef, right, comps, 2, layers - 2, scale=scale, step=22)
+    sweep(beside0, B, A, coef, right, comps, 3, layers - 3, step=21)
     count = layers1 - 4
 
     def residual_sums(t):
@@ -450,7 +451,7 @@
             sums[c, t, :, pl.ds(0, LANES)] = a
             sums[c, t, :, pl.ds(LANES, LANES)] = b
 
-    over_layers(0, count, 5, residual_sums)
+    over_layers(0, count, 10, residual_sums)
     matrix = matrix_0_1(0.125)
     for c in range(comps):
         value = times(sums[c].reshape(count * MID, 2 * LANES), matrix)
@@ -497,7 +498,7 @@
         out_shape=[
             shaped(comps, layers, rows), shaped(comps, layers, rows),
             shaped(comps, layers1, MID), shaped(comps, layers1, MID),
-            shaped(mine + 2 * EDGES, MID),
+            shaped(mine + 2 * EDGES + SPARE, MID),
         ],
         scratch_shapes=[
             vmem(comps, layers, rows),
@@ -641,8 +642,8 @@
 
     over_layers(0, count, 6, add)
     rights = [(b0, n) for _, b0, _, _, n in comps]
-    sweep_many(beside0, A, B, coef, rights, 1, layers - 1, shift, 8)
-    sweep_many(beside0, B, A, coef, rights, SIDE0, layers - SIDE0, shift, 8)
+    sweep_many(beside0, A, B, coef, rights, 1, layers - 1, shift, 17)
+    sweep_many(beside0, B, A, coef, rights, SIDE0, layers - SIDE0, shift, 16)
 
     writes = []
     for c in range(3):
@@ -747,7 +748,7 @@
     hops = [(i, i - 3 + 6 * (i % 2)) for i in range(count)]
     far = lax.ppermute(sent, axes, [(i, to) for i, to in hops if 0 <= to < count])
     mine = edge // 4
-    beyond = swap_outward(jnp.concatenate([sent[EDGES:], beside[EDGES : EDGES + mine]], axis=0), 1)
+    beyond = swap_outward(jnp.concatenate([sent[EDGES : mine + 2 * EDGES], beside[EDGES : EDGES + mine]], axis=0), 1)
     came, far = lax.optimization_barrier((beyond, far))
     other = swap(came, 1)
     widths = tuple(state[0].shape[0] for state in kept)

time: 94.1 us -> 93.1 us (0.989); the launches traced: 92.8 us -> 92.8 us
  waiting for transfers between devices: 43 us -> 44.5 us
  Pallas kernels: 28.5 us -> 27.4 us
    ppermute x3, waiting for transfers between devices: 0.32 us -> 6.14 us  [swap_outward(): lax.ppermute(array, axes, [(i, to) for i, to in goals if 0 <= to < count])]
    ppermute x1, waiting for transfers between devices: 3.57 us -> 0.14 us  [local(): lax.ppermute(sent, axes, [(i, to) for i, to in hops if 0 <= to < count])]
    ppermute x3, starting transfers between devices: 11.4 us -> 9.45 us  [swap_outward(): lax.ppermute(array, axes, [(i, to) for i, to in goals if 0 <= to < count])]
    ppermute x1, starting transfers between devices: 3.08 us -> 4.74 us  [local(): lax.ppermute(sent, axes, [(i, to) for i, to in hops if 0 <= to < count])]
where the time goes in v3:
time: 93.1 us; the launch traced here: 92.8 us
  waiting for transfers between devices  44.5 us (48%)
  Pallas kernels  27.4 us (29%)
  starting transfers between devices  20.6 us (22%)
    ppermute x7, waiting for transfers between devices, local(): lax.ppermute(sent, 'dev', [(m, m ^ turn) for m in range(members)])  36.3 us
    pallas_call x1, Pallas kernels, up(): pl.pallas_call(functools.partial(up_kernel, total_x, parts), in_specs=[WH...  9.53 us
    ppermute x3, starting transfers between devices, swap_outward(): lax.ppermute(array, axes, [(i, to) for i, to in goals if 0 <= to < count])  9.45 us
    pallas_call x2, Pallas kernels, down(): pl.pallas_call(functools.partial(down_kernel, comp_at, first_field), in_s...  7.04 us
    ppermute x3, waiting for transfers between devices, swap_outward(): lax.ppermute(array, axes, [(i, to) for i, to in goals if 0 <= to < count])  6.14 us
    ppermute x7, starting transfers between devices, local(): lax.ppermute(sent, 'dev', [(m, m ^ turn) for m in range(members)])  5.07 us
    ppermute x1, starting transfers between devices, local(): lax.ppermute(sent, axes, [(i, to) for i, to in hops if 0 <= to < count])  4.74 us
    pallas_call x2, Pallas kernels, assemble(): pl.pallas_call(functools.partial(assemble_kernel, members, fields, sends)...  3.85 us
  transfers between devices with their start and end apart: 17, of which 9 were waited for; matrix products, arithmetic and copies ran while one was open for 0% of the time, Pallas kernels for 15%

profile of v3, /device:TPU:7, one launch (start us, length us, event | category | flops | bytes accessed | tf_op | source)
XLA Modules:
  0.0 92.8 jit_solution(3659098467068893644)
XLA Ops:
  0.0 0.7 collective-permute-start.1
  0.7 1.7 %early.1 = f32[1,2,32,1024]{3,2,1,0:T(8,128)S(1)} custom-call(s32[128]{0:T(128)} %source.9, f32[4,32,1024]{2,1,0:T(8,128)} %viscosity.2, f32[4,3,32,1024]{3,2,1,0:T(8,128)} %velocity.1), custom_call_target="tpu_custom_call" | custom-call | tf_op jit(solution)/shard_map/early/pallas_call | solution.py:272
  2.4 1.6 %load.1 = (f32[4,32,1024]{2,1,0:T(8,128)S(1)}, f32[4,3,32,1024]{3,2,1,0:T(8,128)S(1)}) custom-call(f32[4,32,1024]{2,1,0:T(8,128)} %viscosity.2, f32[4,3,32,1024]{3,2,1,0:T(8,128)} %velocity.1), custom_call_target="tpu_custom_call" | custom-call | tf_op jit(solution)/shard_map/load/pallas_call | solution.py:249
  4.0 0.6 collective-permute-done.refs_2_.viscosity_other
  4.7 0.8 pack.3
  5.5 1.8 %collective-permute-start.8 = (f32[1,2,32,1024]{3,2,1,0:T(8,128)S(1)}, f32[1,2,32,1024]{3,2,1,0:T(8,128)S(1)}, u32[]{:S(2)}, u32[]{:S(2)}) collective-permute-start(f32[1,2,32,1024]{3,2,1,0:T(8,128)S(1)} %get-tuple-element.46), channel_id=1, source_target_pairs={{0,6},{1,7},{2,4},{3,5},{4,2},{5,3},{6,0},{7,1},{8,14},{9,15},{10,... | collective-permute-start | bytes 786440 | tf_op jit(solution)/shard_map/ppermute | solution.py:725
  7.3 0.2 collective-permute-start.9
  7.5 0.7 collective-permute-start.10
  8.2 0.8 pack.2
  9.0 1.8 %collective-permute-start.2 = (f32[2,2,32,1024]{3,2,1,0:T(8,128)S(1)}, f32[2,2,32,1024]{3,2,1,0:T(8,128)S(1)}, u32[]{:S(2)}, u32[]{:S(2)}) collective-permute-start(f32[2,2,32,1024]{3,2,1,0:T(8,128)S(1)} %get-tuple-element.40), channel_id=1, source_target_pairs={{0,6},{1,7},{2,4},{3,5},{4,2},{5,3},{6,0},{7,1},{8,14},{9,15},{10,... | collective-permute-start | bytes 1572872 | tf_op jit(solution)/shard_map/ppermute | solution.py:725
  10.8 0.2 collective-permute-start.3
  11.0 5.3 %collective-permute-done.8.refs_1_ = f32[1,2,32,1024]{3,2,1,0:T(8,128)S(1)} collective-permute-done((f32[1,2,32,1024]{3,2,1,0:T(8,128)S(1)}, f32[1,2,32,1024]{3,2,1,0:T(8,128)S(1)}, u32[]{:S(2)}, u32[]{:S(2)}) %collective-permute-start.8) | collective-permute-done | bytes 262176 | tf_op jit(solution)/shard_map/ppermute | solution.py:725
  16.3 0.3 collective-permute-start.4
  16.6 12.6 %collective-permute-done.9.refs_2_ = f32[2,2,32,1024]{3,2,1,0:T(8,128)S(1)} collective-permute-done((f32[2,2,32,1024]{3,2,1,0:T(8,128)S(1)}, f32[2,2,32,1024]{3,2,1,0:T(8,128)S(1)}, u32[]{:S(2)}, u32[]{:S(2)}) %collective-permute-start.9) | collective-permute-done | bytes 524320 | tf_op jit(solution)/shard_map/ppermute | solution.py:725
  29.2 1.9 %assemble.3 = (f32[2,32,32,128]{3,2,1,0:T(8,128)S(1)}, f32[2,7,32,128]{3,2,1,0:T(8,128)S(1)}, f32[2,7,32,128]{3,2,1,0:T(8,128)S(1)}) custom-call(s32[128]{0:T(128)} %source.9, f32[4,32,1024]{2,1,0:T(8,128)S(1)} %get-tuple-element.38.refs_0_.viscosity, f32[4,3,32,1024]{3,2,1,0:T(8,128)S(1)} %get-tuple-element.39.refs_1_.velocity, ...), custom_call_target="tpu_custom_call" | custom-call | tf_op jit(solution)/shard_map/assemble/pallas_call | solution.py:351
  31.2 3.7 %collective-permute-start.11 = (f32[2,7,32,128]{3,2,1,0:T(8,128)S(1)}, f32[2,7,32,128]{3,2,1,0:T(8,128)S(1)}, u32[]{:S(2)}, u32[]{:S(2)}) collective-permute-start(f32[2,7,32,128]{3,2,1,0:T(8,128)S(1)} %get-tuple-element.50), channel_id=1, source_target_pairs={{1,2},{2,1},{3,4},{4,3},{5,6},{6,5},{7,8},{8,7},{9,10},{10,9},{11,... | collective-permute-start | bytes 688136 | tf_op jit(solution)/shard_map/ppermute | solution.py:733
  35.0 6.3 %collective-permute-done.2.refs_0_ = f32[2,2,32,1024]{3,2,1,0:T(8,128)S(1)} collective-permute-done((f32[2,2,32,1024]{3,2,1,0:T(8,128)S(1)}, f32[2,2,32,1024]{3,2,1,0:T(8,128)S(1)}, u32[]{:S(2)}, u32[]{:S(2)}) %collective-permute-start.2) | collective-permute-done | bytes 524320 | tf_op jit(solution)/shard_map/ppermute | solution.py:725
  41.3 12.0 %collective-permute-done.3.refs_1_ = f32[2,2,32,1024]{3,2,1,0:T(8,128)S(1)} collective-permute-done((f32[2,2,32,1024]{3,2,1,0:T(8,128)S(1)}, f32[2,2,32,1024]{3,2,1,0:T(8,128)S(1)}, u32[]{:S(2)}, u32[]{:S(2)}) %collective-permute-start.3) | collective-permute-done | bytes 524320 | tf_op jit(solution)/shard_map/ppermute | solution.py:725
  53.3 1.9 %assemble.2 = (f32[2,32,32,128]{3,2,1,0:T(8,128)S(1)}, f32[2,7,32,128]{3,2,1,0:T(8,128)S(1)}, f32[2,7,32,128]{3,2,1,0:T(8,128)S(1)}) custom-call(s32[128]{0:T(128)} %source.9, f32[4,32,1024]{2,1,0:T(8,128)S(1)} %get-tuple-element.38.refs_0_.viscosity, f32[4,3,32,1024]{3,2,1,0:T(8,128)S(1)} %get-tuple-element.39.refs_1_.velocity, ...), custom_call_target="tpu_custom_call" | custom-call | tf_op jit(solution)/shard_map/assemble/pallas_call | solution.py:351
  55.3 3.6 %collective-permute-start.5 = (f32[2,7,32,128]{3,2,1,0:T(8,128)S(1)}, f32[2,7,32,128]{3,2,1,0:T(8,128)S(1)}, u32[]{:S(2)}, u32[]{:S(2)}) collective-permute-start(f32[2,7,32,128]{3,2,1,0:T(8,128)S(1)} %get-tuple-element.44), channel_id=1, source_target_pairs={{1,2},{2,1},{3,4},{4,3},{5,6},{6,5},{7,8},{8,7},{9,10},{10,9},{11,... | collective-permute-start | bytes 688136 | tf_op jit(solution)/shard_map/ppermute | solution.py:733
  58.9 0.1 collective-permute-start.6
  59.0 2.1 %viscosity.3 = (f32[6,48,32,128]{3,2,1,0:T(8,128)S(1)}, f32[48,32,128]{2,1,0:T(8,128)S(1)}, f32[48,32,128]{2,1,0:T(8,128)S(1)}, f32[6,24,8,128]{3,2,1,0:T(8,128)...) custom-call(f32[2,32,32,128]{3,2,1,0:T(8,128)S(1)} %get-tuple-element.49.own, ...), custom_call_target="tpu_custom_call" | custom-call | flops 200000000 | bytes 8000000 | tf_op jit(solution)/shard_map/viscosity/pallas_call | solution.py:408
  61.1 2.7 %down.2 = (f32[1,48,32,128]{3,2,1,0:T(8,128)S(1)}, f32[1,48,32,128]{3,2,1,0:T(8,128)S(1)}, f32[1,24,8,128]{3,2,1,0:T(8,128)S(1)}, f32[1,24,8,128]{3,2,1,0:T(8,128)S(1)}, f32[24,8,128]{2,1,0:T(8,128)S(1)}) custom-call(f32[2,32,32,128]{3,2,1,0:T(8,128)S(1)} %get-tuple-element.49.own, f32[2,7,32,128]{3,2,1,0:T(8,128)S(1)} %collective-permute-done.11.beyond, ...), custom_call_target="tpu_custom_call" | custom-call | flops 200000000 | bytes 8000000 | tf_op jit(solution)/shard_map/down/pallas_call | solution.py:494
  63.8 0.7 collective-permute-done.5.beyond
  64.5 4.4 %down.3 = (f32[2,48,32,128]{3,2,1,0:T(8,128)S(1)}, f32[2,48,32,128]{3,2,1,0:T(8,128)S(1)}, f32[2,24,8,128]{3,2,1,0:T(8,128)S(1)}, f32[2,24,8,128]{3,2,1,0:T(8,128)S(1)}, f32[24,8,128]{2,1,0:T(8,128)S(1)}) custom-call(f32[2,32,32,128]{3,2,1,0:T(8,128)S(1)} %get-tuple-element.43.own, f32[2,7,32,128]{3,2,1,0:T(8,128)S(1)} %collective-permute-done.5.beyond, ...), custom_call_target="tpu_custom_call" | custom-call | flops 200000000 | bytes 8000000 | tf_op jit(solution)/shard_map/down/pallas_call | solution.py:494
  68.9 0.5 collective-permute-start.13
  69.4 4.7 %collective-permute-start.15 = (f32[24,8,128]{2,1,0:T(8,128)S(1)}, f32[24,8,128]{2,1,0:T(8,128)S(1)}, u32[]{:S(2)}, u32[]{:S(2)}) collective-permute-start(f32[24,8,128]{2,1,0:T(8,128)S(1)} %get-tuple-element.60.refs_2_), channel_id=1, source_target_pairs={{1,4},{3,6},{4,1},{5,8},{6,3},{7,10},{8,5},{9,12},{10,7},{11,14},{... | collective-permute-start | bytes 294920 | tf_op jit(solution)/shard_map/ppermute | solution.py:749
  74.2 2.1 %collective-permute-start.14 = (f32[22,8,128]{2,1,0:T(8,128)S(1)}, f32[22,8,128]{2,1,0:T(8,128)S(1)}, u32[]{:S(2)}, u32[]{:S(2)}) collective-permute-start(f32[22,8,128]{2,1,0:T(8,128)S(1)} %pad_maximum_fusion), channel_id=1, source_target_pairs={{1,2},{2,1},{3,4},{4,3},{5,6},{6,5},{7,8},{8,7},{9,10},{10,9},{11,... | collective-permute-start | bytes 270344 | tf_op jit(solution)/shard_map/ppermute | solution.py:733
  76.3 0.1 collective-permute-done.15.refs_0_
  76.5 5.4 %collective-permute-done.14.refs_1_ = f32[22,8,128]{2,1,0:T(8,128)S(1)} collective-permute-done((f32[22,8,128]{2,1,0:T(8,128)S(1)}, f32[22,8,128]{2,1,0:T(8,128)S(1)}, u32[]{:S(2)}, u32[]{:S(2)}) %collective-permute-start.14) | collective-permute-done | bytes 90144 | tf_op jit(solution)/shard_map/ppermute | solution.py:733
  81.9 1.3 %collective-permute-done.16.refs_4_ = f32[22,8,128]{2,1,0:T(8,128)S(1)} collective-permute-done((f32[22,8,128]{2,1,0:T(8,128)S(1)}, f32[22,8,128]{2,1,0:T(8,128)S(1)}, u32[]{:S(2)}, u32[]{:S(2)}) %collective-permute-start.16) | collective-permute-done | bytes 90144 | tf_op jit(solution)/shard_map/ppermute | solution.py:729
  83.1 9.5 %up.1 = f32[4,3,32,1024]{3,2,1,0:T(8,128)} custom-call(f32[24,8,128]{2,1,0:T(8,128)S(1)} %collective-permute-done.15.refs_0_, f32[22,8,128]{2,1,0:T(8,128)S(1)} %collective-permute-done.14.refs_1_, f32[24,8,128]{2,1,0:T(8,128)S(1)} %get-tuple-element.60.refs_2_, f32[24,8,128]{2,1,0:T(8,128)S(1)} %collective-permute-done.13.refs_3_, ...), custom_call_target="tpu_custom_call" | custom-call | flops 400000000 | bytes 16000000 | tf_op jit(solution)/shard_map/up/pallas_call | solution.py:680
  (15 shorter events, 0.2 us)
Async XLA Ops:
  0.0 4.7 %collective-permute-start.1 = (f32[4,3,32,1024]{3,2,1,0:T(8,128)}, f32[4,3,32,1024]{3,2,1,0:T(8,128)S(1)}, u32[]{:S(2)}, u32[]{:S(2)}) collective-permute-start(f32[4,3,32,1024]{3,2,1,0:T(8,128)} %velocity.1), channel_id=1, source_target_pairs={{0,1},{1,0},{2,3},{3,2},{4,5},{5,4},{6,7},{7,6},{8,9},{9,8},{10,11... | collective-permute-start | bytes 4718600 | tf_op jit(solution)/shard_map/ppermute | solution.py:711
  0.7 4.0 %collective-permute-start = (f32[4,32,1024]{2,1,0:T(8,128)}, f32[4,32,1024]{2,1,0:T(8,128)S(1)}, u32[]{:S(2)}, u32[]{:S(2)}) collective-permute-start(f32[4,32,1024]{2,1,0:T(8,128)} %viscosity.2), channel_id=1, source_target_pairs={{0,1},{1,0},{2,3},{3,2},{4,5},{5,4},{6,7},{7,6},{8,9},{9,8},{10,11... | collective-permute-start | bytes 1572872 | tf_op jit(solution)/shard_map/ppermute | solution.py:711
  2.4 8.4 %collective-permute-start.7 = (f32[1,2,32,1024]{3,2,1,0:T(8,128)S(1)}, f32[1,2,32,1024]{3,2,1,0:T(8,128)S(1)}, u32[]{:S(2)}, u32[]{:S(2)}) collective-permute-start(f32[1,2,32,1024]{3,2,1,0:T(8,128)S(1)} %early.1), channel_id=1, source_target_pairs={{0,6},{1,7},{2,4},{3,5},{4,2},{5,3},{6,0},{7,1},{8,14},{9,15},{10,... | collective-permute-start | bytes 786440 | tf_op jit(solution)/shard_map/ppermute | solution.py:725
  5.5 10.9 %collective-permute-start.8 = (f32[1,2,32,1024]{3,2,1,0:T(8,128)S(1)}, f32[1,2,32,1024]{3,2,1,0:T(8,128)S(1)}, u32[]{:S(2)}, u32[]{:S(2)}) collective-permute-start(f32[1,2,32,1024]{3,2,1,0:T(8,128)S(1)} %get-tuple-element.46), channel_id=1, source_target_pairs={{0,6},{1,7},{2,4},{3,5},{4,2},{5,3},{6,0},{7,1},{8,14},{9,15},{10,... | collective-permute-start | bytes 786440 | tf_op jit(solution)/shard_map/ppermute | solution.py:725
  7.3 22.0 %collective-permute-start.9 = (f32[2,2,32,1024]{3,2,1,0:T(8,128)S(1)}, f32[2,2,32,1024]{3,2,1,0:T(8,128)S(1)}, u32[]{:S(2)}, u32[]{:S(2)}) collective-permute-start(f32[2,2,32,1024]{3,2,1,0:T(8,128)S(1)} %get-tuple-element.47), channel_id=1, source_target_pairs={{0,4},{1,5},{2,6},{3,7},{4,0},{5,1},{6,2},{7,3},{8,12},{9,13},{10,... | collective-permute-start | bytes 1572872 | tf_op jit(solution)/shard_map/ppermute | solution.py:725
  7.5 21.7 %collective-permute-start.10 = (f32[2,2,32,1024]{3,2,1,0:T(8,128)S(1)}, f32[2,2,32,1024]{3,2,1,0:T(8,128)S(1)}, u32[]{:S(2)}, u32[]{:S(2)}) collective-permute-start(f32[2,2,32,1024]{3,2,1,0:T(8,128)S(1)} %get-tuple-element.48), channel_id=1, source_target_pairs={{0,2},{1,3},{2,0},{3,1},{4,6},{5,7},{6,4},{7,5},{8,10},{9,11},{10,... | collective-permute-start | bytes 1572872 | tf_op jit(solution)/shard_map/ppermute | solution.py:725
  9.0 32.3 %collective-permute-start.2 = (f32[2,2,32,1024]{3,2,1,0:T(8,128)S(1)}, f32[2,2,32,1024]{3,2,1,0:T(8,128)S(1)}, u32[]{:S(2)}, u32[]{:S(2)}) collective-permute-start(f32[2,2,32,1024]{3,2,1,0:T(8,128)S(1)} %get-tuple-element.40), channel_id=1, source_target_pairs={{0,6},{1,7},{2,4},{3,5},{4,2},{5,3},{6,0},{7,1},{8,14},{9,15},{10,... | collective-permute-start | bytes 1572872 | tf_op jit(solution)/shard_map/ppermute | solution.py:725
  10.8 42.6 %collective-permute-start.3 = (f32[2,2,32,1024]{3,2,1,0:T(8,128)S(1)}, f32[2,2,32,1024]{3,2,1,0:T(8,128)S(1)}, u32[]{:S(2)}, u32[]{:S(2)}) collective-permute-start(f32[2,2,32,1024]{3,2,1,0:T(8,128)S(1)} %get-tuple-element.41), channel_id=1, source_target_pairs={{0,4},{1,5},{2,6},{3,7},{4,0},{5,1},{6,2},{7,3},{8,12},{9,13},{10,... | collective-permute-start | bytes 1572872 | tf_op jit(solution)/shard_map/ppermute | solution.py:725
  16.3 37.0 %collective-permute-start.4 = (f32[2,2,32,1024]{3,2,1,0:T(8,128)S(1)}, f32[2,2,32,1024]{3,2,1,0:T(8,128)S(1)}, u32[]{:S(2)}, u32[]{:S(2)}) collective-permute-start(f32[2,2,32,1024]{3,2,1,0:T(8,128)S(1)} %get-tuple-element.42), channel_id=1, source_target_pairs={{0,2},{1,3},{2,0},{3,1},{4,6},{5,7},{6,4},{7,5},{8,10},{9,11},{10,... | collective-permute-start | bytes 1572872 | tf_op jit(solution)/shard_map/ppermute | solution.py:725
  31.2 27.8 %collective-permute-start.11 = (f32[2,7,32,128]{3,2,1,0:T(8,128)S(1)}, f32[2,7,32,128]{3,2,1,0:T(8,128)S(1)}, u32[]{:S(2)}, u32[]{:S(2)}) collective-permute-start(f32[2,7,32,128]{3,2,1,0:T(8,128)S(1)} %get-tuple-element.50), channel_id=1, source_target_pairs={{1,2},{2,1},{3,4},{4,3},{5,6},{6,5},{7,8},{8,7},{9,10},{10,9},{11,... | collective-permute-start | bytes 688136 | tf_op jit(solution)/shard_map/ppermute | solution.py:733
  34.9 24.1 %collective-permute-start.12 = (f32[2,7,32,128]{3,2,1,0:T(8,128)S(1)}, f32[2,7,32,128]{3,2,1,0:T(8,128)S(1)}, u32[]{:S(2)}, u32[]{:S(2)}) collective-permute-start(f32[2,7,32,128]{3,2,1,0:T(8,128)S(1)} %get-tuple-element.51), channel_id=1, source_target_pairs={{0,1},{1,0},{2,3},{3,2},{4,5},{5,4},{6,7},{7,6},{8,9},{9,8},{10,11... | collective-permute-start | bytes 688136 | tf_op jit(solution)/shard_map/ppermute | solution.py:729
  55.3 9.2 %collective-permute-start.5 = (f32[2,7,32,128]{3,2,1,0:T(8,128)S(1)}, f32[2,7,32,128]{3,2,1,0:T(8,128)S(1)}, u32[]{:S(2)}, u32[]{:S(2)}) collective-permute-start(f32[2,7,32,128]{3,2,1,0:T(8,128)S(1)} %get-tuple-element.44), channel_id=1, source_target_pairs={{1,2},{2,1},{3,4},{4,3},{5,6},{6,5},{7,8},{8,7},{9,10},{10,9},{11,... | collective-permute-start | bytes 688136 | tf_op jit(solution)/shard_map/ppermute | solution.py:733
  58.9 5.6 %collective-permute-start.6 = (f32[2,7,32,128]{3,2,1,0:T(8,128)S(1)}, f32[2,7,32,128]{3,2,1,0:T(8,128)S(1)}, u32[]{:S(2)}, u32[]{:S(2)}) collective-permute-start(f32[2,7,32,128]{3,2,1,0:T(8,128)S(1)} %get-tuple-element.45), channel_id=1, source_target_pairs={{0,1},{1,0},{2,3},{3,2},{4,5},{5,4},{6,7},{7,6},{8,9},{9,8},{10,11... | collective-permute-start | bytes 688136 | tf_op jit(solution)/shard_map/ppermute | solution.py:729
  68.9 5.3 %collective-permute-start.13 = (f32[24,8,128]{2,1,0:T(8,128)S(1)}, f32[24,8,128]{2,1,0:T(8,128)S(1)}, u32[]{:S(2)}, u32[]{:S(2)}) collective-permute-start(f32[24,8,128]{2,1,0:T(8,128)S(1)} %get-tuple-element.60.refs_2_), channel_id=1, source_target_pairs={{0,1},{1,0},{2,3},{3,2},{4,5},{5,4},{6,7},{7,6},{8,9},{9,8},{10,11... | collective-permute-start | bytes 294920 | tf_op jit(solution)/shard_map/ppermute | solution.py:729
  69.4 7.0 %collective-permute-start.15 = (f32[24,8,128]{2,1,0:T(8,128)S(1)}, f32[24,8,128]{2,1,0:T(8,128)S(1)}, u32[]{:S(2)}, u32[]{:S(2)}) collective-permute-start(f32[24,8,128]{2,1,0:T(8,128)S(1)} %get-tuple-element.60.refs_2_), channel_id=1, source_target_pairs={{1,4},{3,6},{4,1},{5,8},{6,3},{7,10},{8,5},{9,12},{10,7},{11,14},{... | collective-permute-start | bytes 294920 | tf_op jit(solution)/shard_map/ppermute | solution.py:749
  74.2 7.6 %collective-permute-start.14 = (f32[22,8,128]{2,1,0:T(8,128)S(1)}, f32[22,8,128]{2,1,0:T(8,128)S(1)}, u32[]{:S(2)}, u32[]{:S(2)}) collective-permute-start(f32[22,8,128]{2,1,0:T(8,128)S(1)} %pad_maximum_fusion), channel_id=1, source_target_pairs={{1,2},{2,1},{3,4},{4,3},{5,6},{6,5},{7,8},{8,7},{9,10},{10,9},{11,... | collective-permute-start | bytes 270344 | tf_op jit(solution)/shard_map/ppermute | solution.py:733
  81.9 1.3 %collective-permute-start.16 = (f32[22,8,128]{2,1,0:T(8,128)S(1)}, f32[22,8,128]{2,1,0:T(8,128)S(1)}, u32[]{:S(2)}, u32[]{:S(2)}) collective-permute-start(f32[22,8,128]{2,1,0:T(8,128)S(1)} %collective-permute-done.14.refs_1_), channel_id=1, source_target_pairs={{0,1},{1,0},{2,3},{3,2},{4,5},{5,4},{6,7},{7,6},{8,9},{9,8},{10,11... | collective-permute-start | bytes 270344 | tf_op jit(solution)/shard_map/ppermute | solution.py:729
